TPU v7x, 32 devices: a whole 2x2x4 slice. The times are simulated.
32 devices in a mesh: dp: 8 (over z, y), tensor: 4 (over x, core).
Axes of the slice: x: 2, y: 2, z: 4, core: 2. Of those that a mesh axis runs over, the one named last changes fastest.
Arguments:
- tokens: bfloat16 [16384, 768], P(('dp', 'tensor')), may hold values from -6 to 6
- doc_lengths: int32 [32, 8], P('dp'), may hold values from 0 to 512, as said below
- qkv_weight: bfloat16 [768, 2304], P(None, 'tensor'), may hold values from -0.21875 to 0.21875
- attn_out_weight: bfloat16 [768, 768], P('tensor'), may hold values from -1.25 to 1.25
- norm1_gain: float32 [768], replicated, may hold values from 0.5 to 1.5
- norm1_bias: float32 [768], replicated, may hold values from -0.8 to 0.8
- ffn_in_weight: bfloat16 [768, 3072], P(None, 'tensor'), may hold values from -0.21875 to 0.21875
- ffn_out_weight: bfloat16 [3072, 768], P('tensor'), may hold values from -0.109375 to 0.109375
- norm2_gain: float32 [768], replicated, may hold values from 0.5 to 1.5
- norm2_bias: float32 [768], replicated, may hold values from -0.8 to 0.8
- adapter_down: bfloat16 [16, 768, 48], P(None, ('dp', 'tensor')), may hold values from -0.21875 to 0.21875
- adapter_up: bfloat16 [16, 48, 768], P(None, None, ('dp', 'tensor')), may hold values from -1.75 to 1.75
- merging_query: bfloat16 [768, 768], P(('dp', 'tensor')), may hold values from -0.4375 to 0.4375
- merging_key: bfloat16 [768, 768], P(('dp', 'tensor')), may hold values from -0.21875 to 0.21875
- merging_value: bfloat16 [768, 768], P(('dp', 'tensor')), may hold values from -0.21875 to 0.21875
- merging_gain: float32 [768], replicated, may hold values from 0.5 to 1.5
- merging_bias: float32 [768], replicated, may hold values from -0.8 to 0.8
- out_grad: bfloat16 [16384, 768], P(('dp', 'tensor')), may hold values from -6 to 6
Outputs:
- layer_out: float32 [16384, 768], P(('dp', 'tensor'))
- input_grad: float32 [16384, 768], P(('dp', 'tensor'))
- grad_query: float32 [768, 768], P(('dp', 'tensor'))
- grad_key: float32 [768, 768], P(('dp', 'tensor'))
- grad_value: float32 [768, 768], P(('dp', 'tensor'))
- grad_gain: float32 [768], replicated
- grad_bias: float32 [768], replicated
- adapter_mass: float32 [16], replicated
Inputs may be any that keep to these rules, and one draw needn't show every extreme that they name: `doc_lengths`: A row's 8 lengths, some of which may be 0, sum to at most 512; the slots past the sum are padding. Some row holds one document of 512 tokens.
All inputs are finite; a program needn't handle non-finite values.
Results may differ from a plain program's by a relative error of at most 0.04.
Values may be sent and summed in bfloat16 or wider, within the bound.
No kernel may reach another device: no remote copies, remote signals or barrier semaphores. Data moves between devices by JAX's collectives and lax.ppermute only.
A program may use at most 192 MiB of HBM per device.

v0:
```python
import jax
import jax.numpy as jnp
from jax import lax
from jax.sharding import PartitionSpec as P

HEAD_DIM = 64
SEQ = 512
MIX_BLOCK = 128


root_half = 0.7071067811865476
root_tau = 0.3989422804014327
big_negative = -1e30


def gelu_value(argument):
    return 0.5 * argument * (1.0 + lax.erf(argument * root_half))


def gelu_slope(argument):
    return (
        0.5 * (1.0 + lax.erf(argument * root_half))
        + argument * jnp.exp(-0.5 * argument * argument) * root_tau
    )


def normalize(argument):
    centre = jnp.mean(argument, axis=-1, keepdims=True)
    centered = argument - centre
    inv_std = lax.rsqrt(jnp.mean(centered * centered, axis=-1, keepdims=True) + 1e-12)
    return (centered * inv_std, inv_std)


def norm_back(grad_normed, normed, inv_std):
    return inv_std * (
        grad_normed
        - jnp.mean(grad_normed, axis=-1, keepdims=True)
        - normed * jnp.mean(grad_normed * normed, axis=-1, keepdims=True)
    )


def segment_info(lengths):
    doc_ends = jnp.cumsum(lengths, axis=1)
    position = jnp.arange(SEQ, dtype=jnp.int32)
    segment = jnp.sum((position[None, :, None] >= doc_ends[:, None, :]).astype(jnp.int32), axis=2)
    valid = position[None, :] < doc_ends[:, -1:]
    return (segment, valid)


def contract_last(left_side, right_side):
    return lax.dot_general(
        left_side, right_side, (((1,), (1,)), ((), ())), preferred_element_type=jnp.float32
    )


def contract_first(left_side, right_side):
    return lax.dot_general(
        left_side, right_side, (((0,), (0,)), ((), ())), preferred_element_type=jnp.float32
    )


def row_scores(row_block, segment):
    queries = row_block[:, :, 0]
    key_rows = row_block[:, :, 1]
    scores = jnp.einsum(
        "qhd,khd->hqk", queries, key_rows, preferred_element_type=jnp.float32
    ) * HEAD_DIM ** (-0.5)
    same_doc = segment[:, None] == segment[None, :]
    return jnp.where(same_doc[None], scores, big_negative)


def attend_forward(pieces):
    row_block, segment = pieces
    scores = row_scores(row_block, segment)
    row_top = jnp.max(scores, axis=2, keepdims=True)
    exponent = jnp.exp(scores - row_top)
    row_total = jnp.sum(exponent, axis=2, keepdims=True)
    attn_prob = (exponent / row_total).astype(jnp.bfloat16)
    attended = jnp.einsum(
        "hqk,khd->qhd", attn_prob, row_block[:, :, 2], preferred_element_type=jnp.float32
    )
    flat = attended.astype(jnp.bfloat16).reshape(
        attended.shape[0], attended.shape[1] * attended.shape[2]
    )
    return (flat, (row_top + jnp.log(row_total))[:, :, 0])


def attend_back(pieces):
    row_block, segment, log_total, grad_flat = pieces
    queries = row_block[:, :, 0]
    key_rows = row_block[:, :, 1]
    value_rows = row_block[:, :, 2]
    scores = row_scores(row_block, segment)
    attn_prob = jnp.exp(scores - log_total[:, :, None])
    prob_low = attn_prob.astype(jnp.bfloat16)
    grad_out = grad_flat.reshape(queries.shape)
    grad_values = jnp.einsum("hqk,qhd->khd", prob_low, grad_out, preferred_element_type=jnp.float32)
    grad_prob = jnp.einsum("qhd,khd->hqk", grad_out, value_rows, preferred_element_type=jnp.float32)
    row_dot = jnp.sum(grad_prob * attn_prob, axis=2, keepdims=True)
    grad_scores = (attn_prob * (grad_prob - row_dot)).astype(jnp.bfloat16)
    grad_queries = jnp.einsum(
        "hqk,khd->qhd", grad_scores, key_rows, preferred_element_type=jnp.float32
    ) * HEAD_DIM ** (-0.5)
    grad_keys = jnp.einsum(
        "hqk,qhd->khd", grad_scores, queries, preferred_element_type=jnp.float32
    ) * HEAD_DIM ** (-0.5)
    stacked = jnp.stack([grad_queries, grad_keys, grad_values], axis=2).astype(jnp.bfloat16)
    return stacked.reshape(stacked.shape[0], stacked.shape[1] * 3 * stacked.shape[3])


def per_device(
    tokens,
    doc_lengths,
    qkv_weight,
    attn_out_weight,
    norm1_gain,
    norm1_bias,
    ffn_in_weight,
    ffn_out_weight,
    norm2_gain,
    norm2_bias,
    adapter_down,
    adapter_up,
    merging_query,
    merging_key,
    merging_value,
    merging_gain,
    merging_bias,
    out_grad,
):
    own_count = tokens.shape[0]
    features = tokens.shape[1]
    tensor_pos = lax.axis_index("tensor")
    own_start = tensor_pos * own_count
    down_full, up_full, query_full, key_full, value_full = (
        lax.all_gather(adapter_down, ("dp", "tensor"), axis=1, tiled=True),
        lax.all_gather(adapter_up, ("dp", "tensor"), axis=2, tiled=True),
        lax.all_gather(merging_query, ("dp", "tensor"), axis=0, tiled=True),
        lax.all_gather(merging_key, ("dp", "tensor"), axis=0, tiled=True),
        lax.all_gather(merging_value, ("dp", "tensor"), axis=0, tiled=True),
    )
    segment_all, valid_all = segment_info(doc_lengths)
    keep_mask = lax.dynamic_slice_in_dim(valid_all.reshape(-1), own_start, own_count, 0).astype(
        jnp.float32
    )
    proj_weight, attn_weight, inner_weight, outer_weight = (
        qkv_weight,
        attn_out_weight,
        ffn_in_weight,
        ffn_out_weight,
    )
    row_tokens = lax.all_gather(tokens, "tensor", axis=0, tiled=True)
    rows_total = row_tokens.shape[0]
    heads_here = proj_weight.shape[1] // (3 * HEAD_DIM)
    projected = jnp.dot(row_tokens, proj_weight, preferred_element_type=jnp.float32).astype(
        jnp.bfloat16
    )
    row_blocks = projected.reshape(rows_total // SEQ, SEQ, heads_here, 3, HEAD_DIM)
    attended, log_total = lax.map(attend_forward, (row_blocks, segment_all))
    attended_flat = attended.reshape(rows_total, heads_here * HEAD_DIM)
    attn_rows = lax.psum(
        jnp.dot(attended_flat, attn_weight, preferred_element_type=jnp.float32), "tensor"
    )
    normed_rows, inv_rows = normalize(row_tokens.astype(jnp.float32) + attn_rows)
    first_all = normed_rows * norm1_gain + norm1_bias
    first_rows = first_all.astype(jnp.bfloat16)
    normed1 = lax.dynamic_slice_in_dim(normed_rows, own_start, own_count, 0)
    inv_std1 = lax.dynamic_slice_in_dim(inv_rows, own_start, own_count, 0)
    first_own = lax.dynamic_slice_in_dim(first_all, own_start, own_count, 0)
    pre_act = jnp.dot(first_rows, inner_weight, preferred_element_type=jnp.float32)
    ffn_act = gelu_value(pre_act).astype(jnp.bfloat16)
    ffn_own = lax.psum_scatter(
        jnp.dot(ffn_act, outer_weight, preferred_element_type=jnp.float32),
        "tensor",
        scatter_dimension=0,
        tiled=True,
    )
    normed2, inv_std2 = normalize(first_own + ffn_own)
    second = normed2 * norm2_gain + norm2_bias
    logit_scale = features ** (-0.5)
    cotangent = out_grad.astype(jnp.float32) * keep_mask[:, None]

    def mixing_block(running, pieces):
        grad_q, grad_k, grad_v, gain_sum, bias_sum, mass_sum = running
        states, cot_block, keep_block = pieces
        states_low = states.astype(jnp.bfloat16)
        middle = jnp.einsum(
            "td,adr->tar", states_low, down_full, preferred_element_type=jnp.float32
        )
        adapt_act = gelu_value(middle).astype(jnp.bfloat16)
        adapted = (
            states[:, None, :]
            + jnp.einsum("tar,ard->tad", adapt_act, up_full, preferred_element_type=jnp.float32)
        ).astype(jnp.bfloat16)
        fquery = jnp.dot(states_low, query_full, preferred_element_type=jnp.float32).astype(
            jnp.bfloat16
        )
        probe_low = contract_last(fquery, key_full).astype(jnp.bfloat16)
        logits = (
            jnp.einsum("td,tad->ta", probe_low, adapted, preferred_element_type=jnp.float32)
            * logit_scale
        )
        logit_top = jnp.max(logits, axis=1, keepdims=True)
        exponent = jnp.exp(logits - logit_top)
        mix = exponent / jnp.sum(exponent, axis=1, keepdims=True)
        mix_low = mix.astype(jnp.bfloat16)
        blended = jnp.einsum(
            "ta,tad->td", mix_low, adapted, preferred_element_type=jnp.float32
        ).astype(jnp.bfloat16)
        mixed_in = states + jnp.dot(blended, value_full, preferred_element_type=jnp.float32)
        normed3, inv_std3 = normalize(mixed_in)
        block_out = normed3 * merging_gain + merging_bias
        mass_sum = mass_sum + jnp.sum(mix * keep_block[:, None], axis=0)
        gain_sum = gain_sum + jnp.sum(cot_block * normed3, axis=0)
        bias_sum = bias_sum + jnp.sum(cot_block, axis=0)
        grad_pre = norm_back(cot_block * merging_gain, normed3, inv_std3)
        grad_proj = grad_pre.astype(jnp.bfloat16)
        grad_v = grad_v + contract_first(blended, grad_proj)
        grad_blend = contract_last(grad_proj, value_full).astype(jnp.bfloat16)
        grad_mix = jnp.einsum("td,tad->ta", grad_blend, adapted, preferred_element_type=jnp.float32)
        grad_logits = (mix * (grad_mix - jnp.sum(grad_mix * mix, axis=1, keepdims=True))).astype(
            jnp.bfloat16
        )
        grad_probe = (
            jnp.einsum("ta,tad->td", grad_logits, adapted, preferred_element_type=jnp.float32)
            * logit_scale
        ).astype(jnp.bfloat16)
        grad_adapted = (
            mix_low.astype(jnp.float32)[:, :, None] * grad_blend.astype(jnp.float32)[:, None, :]
            + grad_logits.astype(jnp.float32)[:, :, None]
            * probe_low.astype(jnp.float32)[:, None, :]
            * logit_scale
        ).astype(jnp.bfloat16)
        grad_k = grad_k + contract_first(grad_probe, fquery)
        grad_fquery = jnp.dot(grad_probe, key_full, preferred_element_type=jnp.float32).astype(
            jnp.bfloat16
        )
        grad_q = grad_q + contract_first(states_low, grad_fquery)
        grad_states = (
            grad_pre
            + contract_last(grad_fquery, query_full)
            + jnp.sum(grad_adapted, axis=1, dtype=jnp.float32)
        )
        grad_act = jnp.einsum(
            "tad,ard->tar", grad_adapted, up_full, preferred_element_type=jnp.float32
        )
        grad_middle = (grad_act * gelu_slope(middle)).astype(jnp.bfloat16)
        grad_states = grad_states + jnp.einsum(
            "tar,adr->td", grad_middle, down_full, preferred_element_type=jnp.float32
        )
        return ((grad_q, grad_k, grad_v, gain_sum, bias_sum, mass_sum), (block_out, grad_states))

    block_count = own_count // MIX_BLOCK
    square_zero = jnp.zeros((features, features), jnp.float32)
    line_zero = jnp.zeros((features,), jnp.float32)
    start_state = (
        square_zero,
        square_zero,
        square_zero,
        line_zero,
        line_zero,
        jnp.zeros((down_full.shape[0],), jnp.float32),
    )
    running, (block_outs, grad_blocks) = lax.scan(
        mixing_block,
        start_state,
        (
            second.reshape(block_count, MIX_BLOCK, features),
            cotangent.reshape(block_count, MIX_BLOCK, features),
            keep_mask.reshape(block_count, MIX_BLOCK),
        ),
    )
    layer_out = block_outs.reshape(own_count, features)
    grad_second = grad_blocks.reshape(own_count, features)
    grad_sum2 = norm_back(grad_second * norm2_gain, normed2, inv_std2)
    grad_sum2_low = grad_sum2.astype(jnp.bfloat16)
    grad_rows = lax.all_gather(grad_sum2_low, "tensor", axis=0, tiled=True)
    grad_pre_act = (contract_last(grad_rows, outer_weight) * gelu_slope(pre_act)).astype(
        jnp.bfloat16
    )
    grad_first = lax.psum_scatter(
        contract_last(grad_pre_act, inner_weight), "tensor", scatter_dimension=0, tiled=True
    )
    grad_first = grad_first + grad_sum2
    grad_sum1 = norm_back(grad_first * norm1_gain, normed1, inv_std1)
    grad_sum1_low = grad_sum1.astype(jnp.bfloat16)
    grad_attn_rows = lax.all_gather(grad_sum1_low, "tensor", axis=0, tiled=True)
    grad_attended = contract_last(grad_attn_rows, attn_weight).astype(jnp.bfloat16)
    grad_attended = grad_attended.reshape(rows_total // SEQ, SEQ, heads_here * HEAD_DIM)
    grad_projected = lax.map(attend_back, (row_blocks, segment_all, log_total, grad_attended))
    grad_projected = grad_projected.reshape(rows_total, 3 * heads_here * HEAD_DIM)
    grad_tokens = lax.psum_scatter(
        contract_last(grad_projected, proj_weight), "tensor", scatter_dimension=0, tiled=True
    )
    input_grad = grad_tokens + grad_sum1
    grad_q, grad_k, grad_v, gain_sum, bias_sum, mass_sum = running
    token_count = jnp.sum(keep_mask)
    part_query, part_key, part_value = (
        lax.psum_scatter(grad_q, ("dp", "tensor"), scatter_dimension=0, tiled=True),
        lax.psum_scatter(grad_k, ("dp", "tensor"), scatter_dimension=0, tiled=True),
        lax.psum_scatter(grad_v, ("dp", "tensor"), scatter_dimension=0, tiled=True),
    )
    total_gain, total_bias, total_mass, total_count = lax.psum(
        (gain_sum, bias_sum, mass_sum, token_count), ("dp", "tensor")
    )
    return (
        layer_out,
        input_grad,
        part_query,
        part_key,
        part_value,
        total_gain,
        total_bias,
        total_mass / total_count,
    )


def solution(mesh):
    in_specs = (
        P(("dp", "tensor"), None),
        P("dp", None),
        P(None, "tensor"),
        P("tensor", None),
        P(),
        P(),
        P(None, "tensor"),
        P("tensor", None),
        P(),
        P(),
        P(None, ("dp", "tensor"), None),
        P(None, None, ("dp", "tensor")),
        P(("dp", "tensor"), None),
        P(("dp", "tensor"), None),
        P(("dp", "tensor"), None),
        P(),
        P(),
        P(("dp", "tensor"), None),
    )
    out_specs = (
        P(("dp", "tensor"), None),
        P(("dp", "tensor"), None),
        P(("dp", "tensor"), None),
        P(("dp", "tensor"), None),
        P(("dp", "tensor"), None),
        P(),
        P(),
        P(),
    )
    return jax.shard_map(
        per_device, mesh=mesh, in_specs=in_specs, out_specs=out_specs, check_vma=False
    )
```

profile of v0, /device:TPU:0, one launch (start us, length us, event | category | flops | bytes accessed | tf_op | source)
XLA Modules:
  0.0 1181.6 jit_solution(3512707879995927284)
XLA Ops:
  9.8 31.9 %all-gather.9.cloned.1.call-done = bf16[2048,768]{1,0:T(8,128)(2,1)} async-done(((bf16[512,768]{1,0:T(8,128)(2,1)}), bf16[2048,768]{1,0:T(8,128)(2,1)}) %all-gather.9.cloned.1.call-update) | async-done | bytes 3145744 | tf_op jit(solution)/shard_map/all_gather | solution.py:152
  51.0 16.6 %while.47 = (s32[]{:T(128)}, bf16[4,512,192]{1,2,0:T(8,128)(2,1)}, f32[4,3,512]{2,1,0:T(4,128)}, bf16[4,512,3,3,64]{1,4,2,3,0:T(8,128)(2,1)S(1)}, s32[4,512]{1,0:T(4,128)S(1)}, /*index=5*/s32[]{:T(128)}) while((s32[]{:T(128)}, bf16[4,512,192]{1,2,0:T(8,128)(2,1)}, f32[4,3,512]{2,1,0:T(4,128)}, bf16[4,512,3,3,64]{1,4,2,3,0:T(8,128)(2,1)S(1)}, ...), condition=%wide.region_5.6_spmd, body=%wide.region_2.5_spmd.sunk | while | flops 211122688 | bytes 12907597 | solution.py:159
  69.5 4.6 fusion.110
  76.6 126.7 %all-reduce.3.cloned.1.call-done = f32[2048,768]{1,0:T(8,128)} async-done(((f32[2048,768]{1,0:T(8,128)}), f32[2048,768]{1,0:T(8,128)}) %all-reduce.3.cloned.1.call-update) | async-done | bytes 6291472 | tf_op jit(solution)/shard_map/psum | solution.py:161
  203.4 4.6 fusion.91
  220.0 5.0 fusion.87
  233.8 16.9 %all-gather.17.cloned.1.call-done = bf16[16,48,768]{1,0,2:T(8,128)(2,1)} async-done(((bf16[16,48,24]{1,0,2:T(8,128)(2,1)}), bf16[16,48,768]{1,0,2:T(8,128)(2,1)}) %all-gather.17.cloned.1.call-update) | async-done | bytes 1179664 | tf_op jit(solution)/shard_map/all_gather | solution.py:137
  250.7 4.9 copy.82
  255.5 28.2 %reduce-scatter.7.cloned.1.call-done = f32[512,768]{1,0:T(8,128)} async-done(((f32[2048,768]{1,0:T(8,128)}), f32[512,768]{1,0:T(8,128)}) %reduce-scatter.7.cloned.1.call-update) | async-done | bytes 1572880 | tf_op jit(solution)/shard_map/reduce_scatter | solution.py:172
  288.5 36.1 %all-gather.11.cloned.1.call-done = bf16[768,768]{1,0:T(8,128)(2,1)} async-done(((bf16[24,768]{1,0:T(8,128)(2,1)}), bf16[768,768]{1,0:T(8,128)(2,1)}) %all-gather.11.cloned.1.call-update) | async-done | bytes 1179664 | tf_op jit(solution)/shard_map/all_gather | solution.py:138
  324.6 56.4 %all-gather.13.cloned.1.call-done = bf16[768,768]{1,0:T(8,128)(2,1)} async-done(((bf16[24,768]{1,0:T(8,128)(2,1)}), bf16[768,768]{1,0:T(8,128)(2,1)}) %all-gather.13.cloned.1.call-update) | async-done | bytes 1179664 | tf_op jit(solution)/shard_map/all_gather | solution.py:139
  381.0 56.4 %all-gather.19.cloned.1.call-done = bf16[768,768]{1,0:T(8,128)(2,1)} async-done(((bf16[24,768]{1,0:T(8,128)(2,1)}), bf16[768,768]{1,0:T(8,128)(2,1)}) %all-gather.19.cloned.1.call-update) | async-done | bytes 1179664 | tf_op jit(solution)/shard_map/all_gather | solution.py:140
  437.4 186.8 %while.49 = (s32[]{:T(128)}, f32[768,768]{1,0:T(8,128)}, f32[768,768]{1,0:T(8,128)}, f32[768,768]{1,0:T(8,128)}, f32[768]{0:T(1024)}, /*index=5*/f32[768]{0:T(10...) while((s32[]{:T(128)}, f32[768,768]{1,0:T(8,128)}, ...), condition=%wide.region_24.25_spmd.clone, body=%wide.region_12.24_spmd.clone.sunk | while | flops 2006732032 | bytes 173245440 | solution.py:264
  629.1 27.5 %all-gather.21.cloned.1.call-done = bf16[2048,768]{1,0:T(8,128)(2,1)} async-done(((bf16[512,768]{1,0:T(8,128)(2,1)}), bf16[2048,768]{1,0:T(8,128)(2,1)}) %all-gather.21.cloned.1.call-update) | async-done | bytes 3145744 | tf_op jit(solution)/shard_map/all_gather | solution.py:277
  656.6 10.0 fusion.92
  667.5 57.7 %reduce-scatter.9.cloned.1.call-done = f32[512,768]{1,0:T(8,128)} async-done(((f32[2048,768]{1,0:T(8,128)}), f32[512,768]{1,0:T(8,128)}) %reduce-scatter.9.cloned.1.call-update) | async-done | bytes 1572880 | tf_op jit(solution)/shard_map/reduce_scatter | solution.py:281
  730.7 28.6 %all-gather.23.cloned.1.call-done = bf16[2048,768]{1,0:T(8,128)(2,1)} async-done(((bf16[512,768]{1,0:T(8,128)(2,1)}), bf16[2048,768]{1,0:T(8,128)(2,1)}) %all-gather.23.cloned.1.call-update) | async-done | bytes 3145744 | tf_op jit(solution)/shard_map/all_gather | solution.py:287
  762.4 31.1 %while.48 = (s32[]{:T(128)}, bf16[4,512,576]{1,2,0:T(8,128)(2,1)}, bf16[4,512,3,3,64]{1,4,2,3,0:T(8,128)(2,1)}, s32[4,512]{1,0:T(4,128)}, f32[4,3,512]{2,1,0:T(4...) while((s32[]{:T(128)}, bf16[4,512,576]{1,2,0:T(8,128)(2,1)}, bf16[4,512,3,3,64]{1,4,2,3,0:T(8,128)(2,1)}, ...), condition=%wide.region_32.33_spmd, body=%wide.region_30.32_spmd.sunk | while | flops 511736320 | bytes 31234652 | solution.py:290
  795.6 4.6 fusion.111
  803.7 39.8 %all-reduce = (f32[768]{0:T(1024)}, f32[768]{0:T(1024)}, f32[16]{0:T(128)S(1)}, f32[]{:T(128)}) all-reduce(f32[768]{0:T(1024)S(1)} %copy-done.46, f32[768]{0:T(1024)S(1)} %copy-done.49, f32[16]{0:T(128)S(1)} %copy-done.66, f32[]{:T(128)} %fusion.94), channel_id=1, replica_groups=mesh['dp'=8,'tensor'=4] {'dp','tensor'}, use_global_device_ids=true, to_apply=%region_37.38 | all-reduce | flops 1553 | bytes 12424 | tf_op jit(solution)/shard_map/psum | solution.py:303
  844.6 14.9 %reduce-scatter.11.cloned.1.call-done = f32[512,768]{1,0:T(8,128)} async-done(((f32[2048,768]{1,0:T(8,128)}), f32[512,768]{1,0:T(8,128)}) %reduce-scatter.11.cloned.1.call-update) | async-done | bytes 1572880 | tf_op jit(solution)/shard_map/reduce_scatter | solution.py:292
  862.8 102.4 %reduce-scatter.13.cloned.1.call-done = f32[24,768]{1,0:T(8,128)} async-done(((f32[768,768]{1,0:T(8,128)}), f32[24,768]{1,0:T(8,128)}) %reduce-scatter.13.cloned.1.call-update) | async-done | bytes 73744 | tf_op jit(solution)/shard_map/reduce_scatter | solution.py:299
  965.2 103.9 %reduce-scatter.15.cloned.1.call-done = f32[24,768]{1,0:T(8,128)} async-done(((f32[768,768]{1,0:T(8,128)}), f32[24,768]{1,0:T(8,128)}) %reduce-scatter.15.cloned.1.call-update) | async-done | bytes 73744 | tf_op jit(solution)/shard_map/reduce_scatter | solution.py:300
  1069.2 104.6 %reduce-scatter.17.cloned.1.call-done = f32[24,768]{1,0:T(8,128)} async-done(((f32[768,768]{1,0:T(8,128)}), f32[24,768]{1,0:T(8,128)}) %reduce-scatter.17.cloned.1.call-update) | async-done | bytes 73744 | tf_op jit(solution)/shard_map/reduce_scatter | solution.py:301
  (731 shorter events, 296.6 us)
Async XLA Ops:
  8.0 212.0 %copy-start = (bf16[768,768]{1,0:T(8,128)(2,1)S(1)}, bf16[768,768]{1,0:T(8,128)(2,1)}, u32[]{:S(2)}) copy-start(bf16[768,768]{1,0:T(8,128)(2,1)} %param.31) | copy-start | bytes 3538948
  8.0 33.7 %all-gather.9.cloned.1.call-start = ((), (), s32[]{:S(2)}) async-start(), calls=%async_computation.6 | async-start | bytes 3932160 | tf_op jit(solution)/shard_map/all_gather | solution.py:152
  8.7 194.6 %all-reduce.3.cloned.1.call-start = ((), (), s32[]{:S(2)}) async-start(), calls=%async_computation.7 | async-start | bytes 12582912 | tf_op jit(solution)/shard_map/psum | solution.py:161
  74.1 155.4 %all-gather.15.cloned.1.call-start = ((), (), s32[]{:S(2)}) async-start(), calls=%async_computation.11 | async-start | bytes 3244032 | tf_op jit(solution)/shard_map/all_gather | solution.py:136
  75.7 175.0 %all-gather.17.cloned.1.call-start = ((), (), s32[]{:S(2)}) async-start(), calls=%async_computation.12 | async-start | bytes 3244032 | tf_op jit(solution)/shard_map/all_gather | solution.py:137
  76.4 207.3 %reduce-scatter.7.cloned.1.call-start = ((), (), s32[]{:S(2)}) async-start(), calls=%async_computation.8 | async-start | bytes 7864320 | tf_op jit(solution)/shard_map/reduce_scatter | solution.py:172
  203.4 6.4 copy-start.28
  225.0 99.6 %all-gather.11.cloned.1.call-start = ((), (), s32[]{:S(2)}) async-start(), calls=%async_computation.9 | async-start | bytes 1216512 | tf_op jit(solution)/shard_map/all_gather | solution.py:138
  225.6 155.4 %all-gather.13.cloned.1.call-start = ((), (), s32[]{:S(2)}) async-start(), calls=%async_computation.10 | async-start | bytes 1216512 | tf_op jit(solution)/shard_map/all_gather | solution.py:139
  226.3 211.1 %all-gather.19.cloned.1.call-start = ((), (), s32[]{:S(2)}) async-start(), calls=%async_computation.13 | async-start | bytes 1216512 | tf_op jit(solution)/shard_map/all_gather | solution.py:140
  227.1 429.6 %all-gather.21.cloned.1.call-start = ((), (), s32[]{:S(2)}) async-start(), calls=%async_computation.14 | async-start | bytes 3932160 | tf_op jit(solution)/shard_map/all_gather | solution.py:277
  255.5 31.5 %copy-start.56 = (f32[768]{0:T(1024)S(1)}, f32[768]{0:T(1024)}, u32[]{:S(2)}) copy-start(f32[768]{0:T(1024)} %param.32) | copy-start | bytes 9220
  255.5 31.5 %copy-start.70 = (f32[768]{0:T(1024)S(1)}, f32[768]{0:T(1024)}, u32[]{:S(2)}) copy-start(f32[768]{0:T(1024)} %param.33) | copy-start | bytes 9220
  285.9 151.5 %copy-start.32 = (f32[768]{0:T(1024)S(1)}, f32[768]{0:T(1024)}, u32[]{:S(2)}) copy-start(f32[768]{0:T(1024)} %param.39) | copy-start | bytes 9220
  287.0 150.4 %copy-start.62 = (f32[512]{0:T(512)}, f32[512]{0:T(512)S(1)}, u32[]{:S(2)}) copy-start(f32[512]{0:T(512)S(1)} %add_rsqrt_fusion.2) | copy-start | bytes 6148
  627.1 29.5 %copy-start.73 = (bf16[768,768]{1,0:T(8,128)(2,1)S(1)}, bf16[768,768]{1,0:T(8,128)(2,1)}, u32[]{:S(2)}) copy-start(bf16[768,768]{1,0:T(8,128)(2,1)} %param.30) | copy-start | bytes 3538948
  629.1 96.1 %reduce-scatter.9.cloned.1.call-start = ((), (), s32[]{:S(2)}) async-start(), calls=%async_computation.15 | async-start | bytes 7864320 | tf_op jit(solution)/shard_map/reduce_scatter | solution.py:281
  666.6 58.6 %copy-start.68 = (f32[768]{0:T(1024)S(1)}, f32[768]{0:T(1024)}, u32[]{:S(2)}) copy-start(f32[768]{0:T(1024)} %param.28) | copy-start | bytes 9220
  666.6 92.7 %all-gather.23.cloned.1.call-start = ((), (), s32[]{:S(2)}) async-start(), calls=%async_computation.16 | async-start | bytes 3932160 | tf_op jit(solution)/shard_map/all_gather | solution.py:287
  727.9 31.4 %copy-start.40 = (bf16[192,768]{1,0:T(8,128)(2,1)S(1)}, bf16[192,768]{1,0:T(8,128)(2,1)}, u32[]{:S(2)}) copy-start(bf16[192,768]{1,0:T(8,128)(2,1)} %param.27) | copy-start | bytes 884740
  730.6 128.8 %reduce-scatter.11.cloned.1.call-start = ((), (), s32[]{:S(2)}) async-start(), calls=%async_computation.17 | async-start | bytes 7864320 | tf_op jit(solution)/shard_map/reduce_scatter | solution.py:292
  800.2 165.0 %reduce-scatter.13.cloned.1.call-start = ((), (), s32[]{:S(2)}) async-start(), calls=%async_computation.18 | async-start | bytes 2433024 | tf_op jit(solution)/shard_map/reduce_scatter | solution.py:299
  801.0 268.2 %reduce-scatter.15.cloned.1.call-start = ((), (), s32[]{:S(2)}) async-start(), calls=%async_computation.19 | async-start | bytes 2433024 | tf_op jit(solution)/shard_map/reduce_scatter | solution.py:300
  801.7 372.1 %reduce-scatter.17.cloned.1.call-start = ((), (), s32[]{:S(2)}) async-start(), calls=%async_computation.20 | async-start | bytes 2433024 | tf_op jit(solution)/shard_map/reduce_scatter | solution.py:301
  (196 other events, 465.0 us)
Sparse Core Ops, SparseCore 0:
  10.4 31.2 all-gather.8
  74.3 129.0 all-reduce.2
  225.1 58.5 reduce-scatter.6
  629.2 27.3 all-gather.20
  666.8 58.3 reduce-scatter.8
  730.7 28.5 all-gather.22
  800.3 59.0 reduce-scatter.10
  866.2 99.0 reduce-scatter.12
  971.1 97.9 reduce-scatter.14
  1075.7 98.0 reduce-scatter.16
Sparse Core Ops, SparseCore 1:
  77.9 102.2 all-gather.14
  183.3 67.3 all-gather.16
  253.9 70.7 all-gather.10
  327.9 53.0 all-gather.12
  384.4 53.0 all-gather.18
where the time goes:
time: 1190 us; the launch traced here: 1180 us
  waiting for transfers between devices  797 us (67%)
  matrix products  170 us (14%)
  local copies, waits for them, and re-layouts  77.9 us (7%)
  other arithmetic  77.3 us (6%)
  blocking collectives  39.8 us (3%)
  between operations  16.5 us (1%)
    psum x1, waiting for transfers between devices, per_device(): lax.psum(jnp.dot(attended_flat, attn_weight, preferred_element_type=jnp.f...  127 us
    reduce_scatter x1, waiting for transfers between devices, per_device(): lax.psum_scatter(grad_v, ('dp', 'tensor'), scatter_dimension=0, tiled=True)  105 us
    reduce_scatter x1, waiting for transfers between devices, per_device(): lax.psum_scatter(grad_k, ('dp', 'tensor'), scatter_dimension=0, tiled=True)  104 us
    reduce_scatter x1, waiting for transfers between devices, per_device(): lax.psum_scatter(grad_q, ('dp', 'tensor'), scatter_dimension=0, tiled=True)  102 us
    reduce_scatter x1, waiting for transfers between devices, per_device(): lax.psum_scatter(contract_last(grad_pre_act, inner_weight), 'tensor', sca...  57.7 us
    all_gather x1, waiting for transfers between devices, per_device(): lax.all_gather(merging_value, ('dp', 'tensor'), axis=0, tiled=True)  56.4 us
    all_gather x1, waiting for transfers between devices, per_device(): lax.all_gather(merging_key, ('dp', 'tensor'), axis=0, tiled=True)  56.4 us
    psum x1, blocking collectives, per_device(): lax.psum((gain_sum, bias_sum, mass_sum, token_count), ('dp', 'tensor'))  39.8 us
  transfers between devices with their start and end apart: 15, of which 14 were waited for; matrix products, arithmetic and copies ran while one was open for 3% of the time, Pallas kernels for 0%

commit v1 on v0

v1 whole, which is shorter than its diff:
```python
import functools

import jax
import jax.numpy as jnp
from jax import lax
from jax.experimental import pallas as pl
from jax.experimental.pallas import tpu as pltpu
from jax.sharding import PartitionSpec as P

HEAD_DIM = 64
AXES = ("dp", "tensor")
VMEM_BYTES = 58 * 1024 * 1024
LANES = 128
EPS = 1e-12
BIG_NEGATIVE = -1e30
ROOT_HALF = 0.7071067811865476
ROOT_TAU = 0.3989422804014327
F32, BF16 = jnp.float32, jnp.bfloat16

SMEM = pl.BlockSpec(memory_space=pltpu.SMEM)
VMEM = pl.BlockSpec(memory_space=pltpu.VMEM)
ANY = pl.BlockSpec(memory_space=pl.ANY)


def dot(a, b):
    return lax.dot_general(a, b, (((1,), (0,)), ((), ())), preferred_element_type=F32)


def dot_last(a, b):
    return lax.dot_general(a, b, (((1,), (1,)), ((), ())), preferred_element_type=F32)


def dot_first(a, b):
    return lax.dot_general(a, b, (((0,), (0,)), ((), ())), preferred_element_type=F32)


def normalize(u):
    centered = u - jnp.mean(u, axis=-1, keepdims=True)
    inv_std = lax.rsqrt(jnp.mean(centered * centered, axis=-1, keepdims=True) + EPS)
    return centered * inv_std, inv_std


def norm_back(grad, normed, inv_std):
    return inv_std * (
        grad
        - jnp.mean(grad, axis=-1, keepdims=True)
        - normed * jnp.mean(grad * normed, axis=-1, keepdims=True)
    )


def gelu_both(u):
    half = 0.5 * (1.0 + lax.erf(u * ROOT_HALF))
    return u * half, half + u * jnp.exp(-0.5 * u * u) * ROOT_TAU


def piece_copies(pieces, place, parity, scratch, sems):
    out = {}
    for i, (piece, (quarter, side)) in enumerate(zip(pieces, place)):
        rows = piece.shape[0]
        if side is None:
            target = scratch.at[quarter]
        else:
            first = parity if side == 0 else 1 - parity
            target = scratch.at[quarter, pl.ds(pl.multiple_of(first * rows, 16), rows)]
        out.setdefault(quarter, []).append(pltpu.make_async_copy(piece, target, sems.at[i]))
    return out


def bring_quarters(step, groups):
    @pl.when(step == 0)
    def _():
        for copies in groups:
            for quarter in sorted(copies):
                for copy in copies[quarter]:
                    copy.start()

    for quarter in range(4):

        @pl.when(step == quarter)
        def _(quarter=quarter):
            for copies in groups:
                for copy in copies[quarter]:
                    copy.wait()


PLACE = ((0, None), (1, None), (2, 0), (2, 1), (3, 0), (3, 1))
N_PIECES = len(PLACE)


def segment_bias(meta_ref, lengths_ref, bias_ref):
    seq = bias_ref.shape[0]
    row = meta_ref[1]
    by_row = lax.broadcasted_iota(jnp.int32, (seq, 1), 0)
    by_lane = lax.broadcasted_iota(jnp.int32, (1, seq), 1)
    seg_row = jnp.zeros((seq, 1), jnp.int32)
    seg_lane = jnp.zeros((1, seq), jnp.int32)
    end = jnp.int32(0)
    for i in range(lengths_ref.shape[1]):
        end = end + lengths_ref[row, i]
        seg_row = seg_row + jnp.where(by_row >= end, 1, 0)
        seg_lane = seg_lane + jnp.where(by_lane >= end, 1, 0)
    bias_ref[...] = jnp.where(seg_row == seg_lane, 0.0, BIG_NEGATIVE).astype(F32)


def attend_forward(*refs):
    meta, lengths, tokens, gain, shift = refs[:5]
    qkv_pieces, out_pieces = refs[5 : 5 + N_PIECES], refs[5 + N_PIECES : 5 + 2 * N_PIECES]
    rest = refs[5 + 2 * N_PIECES :]
    flat_out, turned_out, att_out, prob_out, first_out, normed_out, inv_out = rest[:7]
    qkv_w, out_w, bias, total, sems, out_sems = rest[7:]
    step = pl.program_id(0)
    parity = meta[0]
    bring_quarters(
        step,
        (
            piece_copies(qkv_pieces, PLACE, parity, qkv_w, sems),
            piece_copies(out_pieces, PLACE, parity, out_w, out_sems),
        ),
    )

    @pl.when(step == 0)
    def _():
        segment_bias(meta, lengths, bias)
        total[...] = tokens[...].astype(F32)

    flat = dot(tokens[...], qkv_w[step]).astype(BF16)
    flat_out[0] = flat
    turned = flat.T
    turned_out[0] = turned
    width = 3 * HEAD_DIM
    for head in range(flat.shape[1] // width):
        base = head * width
        keys = flat[:, base + HEAD_DIM : base + 2 * HEAD_DIM]
        queries = turned[base : base + HEAD_DIM] * BF16(HEAD_DIM**-0.5)
        values = turned[base + 2 * HEAD_DIM : base + width]
        scores = dot(keys, queries) + bias[...]
        exponent = jnp.exp(scores - jnp.max(scores, axis=0, keepdims=True))
        prob = (exponent * (1.0 / jnp.sum(exponent, axis=0, keepdims=True))).astype(BF16)
        prob_out[0, head] = prob
        att_out[0, head * HEAD_DIM : (head + 1) * HEAD_DIM] = dot(values, prob).astype(BF16)
    total[...] += dot(att_out[0].T, out_w[step])

    @pl.when(step == 3)
    def _():
        normed, inv_std = normalize(total[...])
        normed_out[...] = normed
        inv_out[...] = inv_std
        first_out[...] = normed * gain[...] + shift[...]


def whole(shape):
    return pl.BlockSpec(shape, lambda i: (0,) * len(shape))


def by_quarter(shape):
    return pl.BlockSpec((1, *shape), lambda i: (i,) + (0,) * len(shape))


def sds(shape, dtype):
    return jax.ShapeDtypeStruct(shape, dtype)


def params(**kw):
    return pltpu.CompilerParams(vmem_limit_bytes=VMEM_BYTES, **kw)


def call_attend_forward(meta, lengths, tokens, gain, shift, qkv_pieces, out_pieces):
    seq, width = tokens.shape
    columns = qkv_pieces[0].shape[1]
    heads = columns // (3 * HEAD_DIM)
    inner = heads * HEAD_DIM
    return pl.pallas_call(
        attend_forward,
        grid=(4,),
        in_specs=[SMEM, SMEM, whole((seq, width)), whole((1, width)), whole((1, width))]
        + [ANY] * (2 * N_PIECES),
        out_specs=[
            by_quarter((seq, columns)),
            by_quarter((columns, seq)),
            by_quarter((inner, seq)),
            by_quarter((heads, seq, seq)),
            whole((seq, width)),
            whole((seq, width)),
            whole((seq, 1)),
        ],
        out_shape=[
            sds((4, seq, columns), BF16),
            sds((4, columns, seq), BF16),
            sds((4, inner, seq), BF16),
            sds((4, heads, seq, seq), BF16),
            sds((seq, width), F32),
            sds((seq, width), F32),
            sds((seq, 1), F32),
        ],
        scratch_shapes=[
            pltpu.VMEM((4, width, columns), BF16),
            pltpu.VMEM((4, inner, width), BF16),
            pltpu.VMEM((seq, seq), F32),
            pltpu.VMEM((seq, width), F32),
            pltpu.SemaphoreType.DMA((N_PIECES,)),
            pltpu.SemaphoreType.DMA((N_PIECES,)),
        ],
        compiler_params=params(),
        name="attend_forward",
    )(meta, lengths, tokens, gain, shift, *qkv_pieces, *out_pieces)


def ffn_forward(*refs):
    meta, first = refs[:2]
    in_pieces, out_pieces = refs[2 : 2 + N_PIECES], refs[2 + N_PIECES : 2 + 2 * N_PIECES]
    slope_out, sum_out, in_w, out_w, low, sems, out_sems = refs[2 + 2 * N_PIECES :]
    step = pl.program_id(0)
    bring_quarters(
        step,
        (
            piece_copies(in_pieces, PLACE, meta[0], in_w, sems),
            piece_copies(out_pieces, PLACE, meta[0], out_w, out_sems),
        ),
    )

    @pl.when(step == 0)
    def _():
        low[...] = first[...].astype(BF16)
        sum_out[...] = first[...]

    value, slope = gelu_both(dot(low[...], in_w[step]))
    slope_out[0] = slope.astype(BF16)
    sum_out[...] += dot(value.astype(BF16), out_w[step])


def call_ffn_forward(meta, first, in_pieces, out_pieces):
    seq, width = first.shape
    hidden = in_pieces[0].shape[1]
    return pl.pallas_call(
        ffn_forward,
        grid=(4,),
        in_specs=[SMEM, whole((seq, width))] + [ANY] * (2 * N_PIECES),
        out_specs=[by_quarter((seq, hidden)), whole((seq, width))],
        out_shape=[sds((4, seq, hidden), BF16), sds((seq, width), F32)],
        scratch_shapes=[
            pltpu.VMEM((4, width, hidden), BF16),
            pltpu.VMEM((4, hidden, width), BF16),
            pltpu.VMEM((seq, width), BF16),
            pltpu.SemaphoreType.DMA((N_PIECES,)),
            pltpu.SemaphoreType.DMA((N_PIECES,)),
        ],
        compiler_params=params(),
        name="ffn_forward",
    )(meta, first, *in_pieces, *out_pieces)


def merging(
    n_adapters,
    meta,
    lengths,
    sums,
    gain2,
    shift2,
    gain3,
    shift3,
    out_grad,
    weights,
    layer_out,
    grad_sum2_out,
    grad_low_out,
    grad_out,
    lines_out,
):
    seq, width = sums.shape
    scale = width**-0.5
    down, up, query, key, value = (weights.at[i] for i in range(5))
    spread = jnp.where(
        lax.broadcasted_iota(jnp.int32, (LANES, width), 0)
        == lax.broadcasted_iota(jnp.int32, (LANES, width), 1) // (width // n_adapters),
        1.0,
        0.0,
    ).astype(BF16)
    real_lane = lax.broadcasted_iota(jnp.int32, (1, LANES), 1) < n_adapters

    def by_adapter(terms):
        high = terms.astype(BF16)
        rest = (terms - high.astype(F32)).astype(BF16)
        return dot_last(high, spread) + dot_last(rest, spread)

    normed2, inv_std2 = normalize(sums[...])
    second = normed2 * gain2[...] + shift2[...]
    second_low = second.astype(BF16)
    middle = dot(second_low, down[...])
    act, slope = gelu_both(middle)
    act = act.astype(BF16).astype(F32)
    fquery = dot(second_low, query[...]).astype(BF16)
    probe = dot_last(fquery, key[...]).astype(BF16)
    probe_up = dot(probe, up[...])
    logits = scale * (
        jnp.sum(probe.astype(F32) * second, axis=1, keepdims=True) + by_adapter(act * probe_up)
    )
    logits = jnp.where(real_lane, logits, BIG_NEGATIVE)
    exponent = jnp.exp(logits - jnp.max(logits, axis=1, keepdims=True))
    mix = exponent / jnp.sum(exponent, axis=1, keepdims=True)
    mix_low = mix.astype(BF16)
    mix_sum = jnp.sum(mix_low.astype(F32), axis=1, keepdims=True)
    mix_wide = dot(mix_low, spread)
    blended = (second * mix_sum + dot_last((mix_wide * act).astype(BF16), up[...])).astype(BF16)
    normed3, inv_std3 = normalize(second + dot(blended, value[...]))
    layer_out[...] = normed3 * gain3[...] + shift3[...]

    count = jnp.int32(0)
    for i in range(lengths.shape[1]):
        count = count + lengths[meta[1], i]
    keep = jnp.where(lax.broadcasted_iota(jnp.int32, (seq, 1), 0) < count, 1.0, 0.0)
    cot = out_grad[...].astype(F32) * keep
    lines_out[...] = jnp.zeros_like(lines_out)
    lines_out[0:1] = jnp.sum(cot * normed3, axis=0, keepdims=True)
    lines_out[1:2] = jnp.sum(cot, axis=0, keepdims=True)
    mass = jnp.sum(mix * keep, axis=0, keepdims=True)
    lane = lax.broadcasted_iota(jnp.int32, (1, LANES), 1)
    lines_out[2:3, :LANES] = jnp.where(lane == n_adapters, jnp.sum(keep), mass)

    grad_pre = norm_back(cot * gain3[...], normed3, inv_std3)
    grad_proj = grad_pre.astype(BF16)
    grad_out[2] = dot_first(blended, grad_proj).astype(grad_out.dtype)
    grad_blend = dot_last(grad_proj, value[...]).astype(BF16)
    blend_up = dot(grad_blend, up[...])
    grad_mix = jnp.sum(grad_blend.astype(F32) * second, axis=1, keepdims=True) + by_adapter(
        act * blend_up
    )
    grad_logits = (mix * (grad_mix - jnp.sum(grad_mix * mix, axis=1, keepdims=True))).astype(BF16)
    logit_sum = jnp.sum(grad_logits.astype(F32), axis=1, keepdims=True)
    logit_wide = dot(grad_logits, spread)
    grad_probe = (
        scale * (second * logit_sum + dot_last((logit_wide * act).astype(BF16), up[...]))
    ).astype(BF16)
    grad_out[1] = dot_first(grad_probe, fquery).astype(grad_out.dtype)
    grad_fquery = dot(grad_probe, key[...]).astype(BF16)
    grad_out[0] = dot_first(second_low, grad_fquery).astype(grad_out.dtype)
    grad_middle = ((mix_wide * blend_up + (scale * logit_wide) * probe_up) * slope).astype(BF16)
    grad_second = (
        grad_pre
        + dot_last(grad_fquery, query[...])
        + grad_blend.astype(F32) * mix_sum
        + probe.astype(F32) * (scale * logit_sum)
        + dot_last(grad_middle, down[...])
    )
    grad_sum2 = norm_back(grad_second * gain2[...], normed2, inv_std2)
    grad_sum2_out[...] = grad_sum2
    grad_low_out[...] = grad_sum2.astype(BF16)


def call_merging(
    n_adapters, meta, lengths, sums, gain2, shift2, gain3, shift3, out_grad, weights, grad_type
):
    seq, width = sums.shape
    return pl.pallas_call(
        functools.partial(merging, n_adapters),
        in_specs=[SMEM, SMEM] + [VMEM] * 7,
        out_specs=[VMEM] * 5,
        out_shape=[
            sds((seq, width), F32),
            sds((seq, width), F32),
            sds((seq, width), BF16),
            sds((3, width, width), grad_type),
            sds((8, width), F32),
        ],
        compiler_params=params(),
        name="merging",
    )(meta, lengths, sums, gain2, shift2, gain3, shift3, out_grad, weights)


def ffn_backward(*refs):
    meta, grad_sum2, grad_low, normed1, inv_std1, gain1, slope = refs[:7]
    in_pieces, out_pieces = refs[7 : 7 + N_PIECES], refs[7 + N_PIECES : 7 + 2 * N_PIECES]
    grad_out, grad_low_out, in_w, out_w, total, sems, out_sems = refs[7 + 2 * N_PIECES :]
    step = pl.program_id(0)
    bring_quarters(
        step,
        (
            piece_copies(out_pieces, PLACE, meta[0], out_w, out_sems),
            piece_copies(in_pieces, PLACE, meta[0], in_w, sems),
        ),
    )

    @pl.when(step == 0)
    def _():
        total[...] = grad_sum2[...]

    grad_pre = (dot_last(grad_low[...], out_w[step]) * slope[0].astype(F32)).astype(BF16)
    total[...] += dot_last(grad_pre, in_w[step])

    @pl.when(step == 3)
    def _():
        grad = norm_back(total[...] * gain1[...], normed1[...], inv_std1[...])
        grad_out[...] = grad
        grad_low_out[...] = grad.astype(BF16)


def call_ffn_backward(
    meta, grad_sum2, grad_low, normed1, inv_std1, gain1, slope, in_pieces, out_pieces
):
    seq, width = grad_sum2.shape
    hidden = in_pieces[0].shape[1]
    return pl.pallas_call(
        ffn_backward,
        grid=(4,),
        in_specs=[
            SMEM,
            whole((seq, width)),
            whole((seq, width)),
            whole((seq, width)),
            whole((seq, 1)),
            whole((1, width)),
            by_quarter((seq, hidden)),
        ]
        + [ANY] * (2 * N_PIECES),
        out_specs=[whole((seq, width)), whole((seq, width))],
        out_shape=[sds((seq, width), F32), sds((seq, width), BF16)],
        scratch_shapes=[
            pltpu.VMEM((4, width, hidden), BF16),
            pltpu.VMEM((4, hidden, width), BF16),
            pltpu.VMEM((seq, width), F32),
            pltpu.SemaphoreType.DMA((N_PIECES,)),
            pltpu.SemaphoreType.DMA((N_PIECES,)),
        ],
        compiler_params=params(),
        name="ffn_backward",
    )(meta, grad_sum2, grad_low, normed1, inv_std1, gain1, slope, *in_pieces, *out_pieces)


def attend_backward(*refs):
    meta, grad_sum1, grad_low, flat_ref, turned_ref, att_ref, prob_ref = refs[:7]
    qkv_pieces, out_pieces = refs[7 : 7 + N_PIECES], refs[7 + N_PIECES : 7 + 2 * N_PIECES]
    input_grad, qkv_w, out_w, grad_turned, sems, out_sems = refs[7 + 2 * N_PIECES :]
    step = pl.program_id(0)
    bring_quarters(
        step,
        (
            piece_copies(out_pieces, PLACE, meta[0], out_w, out_sems),
            piece_copies(qkv_pieces, PLACE, meta[0], qkv_w, sems),
        ),
    )

    @pl.when(step == 0)
    def _():
        input_grad[...] = grad_sum1[...]

    grad_att = dot_last(out_w[step], grad_low[...]).astype(BF16)
    width = 3 * HEAD_DIM
    root = HEAD_DIM**-0.5
    for head in range(att_ref.shape[1] // HEAD_DIM):
        base = head * width
        queries = turned_ref[0, base : base + HEAD_DIM]
        keys = turned_ref[0, base + HEAD_DIM : base + 2 * HEAD_DIM]
        values = flat_ref[0, :, base + 2 * HEAD_DIM : base + width]
        part = slice(head * HEAD_DIM, (head + 1) * HEAD_DIM)
        grad = grad_att[part]
        prob = prob_ref[0, head]
        row_dot = jnp.sum(grad.astype(F32) * att_ref[0, part].astype(F32), axis=0, keepdims=True)
        grad_scores = (prob.astype(F32) * (dot(values, grad) - row_dot)).astype(BF16)
        grad_turned[base : base + HEAD_DIM] = (dot(keys, grad_scores) * root).astype(BF16)
        grad_turned[base + HEAD_DIM : base + 2 * HEAD_DIM] = (
            dot_last(queries, grad_scores) * root
        ).astype(BF16)
        grad_turned[base + 2 * HEAD_DIM : base + width] = dot_last(grad, prob).astype(BF16)
    input_grad[...] += dot_last(grad_turned[...].T, qkv_w[step])


def call_attend_backward(
    meta, grad_sum1, grad_low, flat, turned, att, prob, qkv_pieces, out_pieces
):
    seq, width = grad_sum1.shape
    columns = qkv_pieces[0].shape[1]
    heads = columns // (3 * HEAD_DIM)
    inner = heads * HEAD_DIM
    return pl.pallas_call(
        attend_backward,
        grid=(4,),
        in_specs=[
            SMEM,
            whole((seq, width)),
            whole((seq, width)),
            by_quarter((seq, columns)),
            by_quarter((columns, seq)),
            by_quarter((inner, seq)),
            by_quarter((heads, seq, seq)),
        ]
        + [ANY] * (2 * N_PIECES),
        out_specs=whole((seq, width)),
        out_shape=sds((seq, width), F32),
        scratch_shapes=[
            pltpu.VMEM((4, width, columns), BF16),
            pltpu.VMEM((4, inner, width), BF16),
            pltpu.VMEM((columns, seq), BF16),
            pltpu.SemaphoreType.DMA((N_PIECES,)),
            pltpu.SemaphoreType.DMA((N_PIECES,)),
        ],
        compiler_params=params(),
        name="attend_backward",
    )(meta, grad_sum1, grad_low, flat, turned, att, prob, *qkv_pieces, *out_pieces)


class Hops:
    def __init__(self, mesh):
        self.count = mesh.size
        self.tensor = mesh.shape["tensor"]
        self.dp = mesh.shape["dp"]

    def flip(self, array, bits):
        return lax.ppermute(array, AXES, [(i, i ^ bits) for i in range(self.count)])


def frozen_pieces(hops, weight, parity):
    half = weight.shape[0] // 2
    mine = lax.dynamic_slice_in_dim(weight, parity * half, half, 0)
    across = hops.flip(mine, 2)
    around = hops.flip(across, hops.tensor)
    other = hops.flip(weight, 1)
    return (weight, other, across, around, hops.flip(across, 1), hops.flip(around, 1))


def per_device(
    hops,
    tokens,
    doc_lengths,
    qkv_weight,
    attn_out_weight,
    norm1_gain,
    norm1_bias,
    ffn_in_weight,
    ffn_out_weight,
    norm2_gain,
    norm2_bias,
    adapter_down,
    adapter_up,
    merging_query,
    merging_key,
    merging_value,
    merging_gain,
    merging_bias,
    out_grad,
):
    n_adapters, rows, rank = adapter_down.shape
    parity = lax.axis_index("dp") % 2
    meta = jnp.stack([parity, lax.axis_index("tensor")]).astype(jnp.int32)
    line = lambda v: v[None, :]

    qkv_pieces = frozen_pieces(hops, qkv_weight, parity)
    out_pieces = frozen_pieces(hops, attn_out_weight, parity)
    in_pieces = frozen_pieces(hops, ffn_in_weight, parity)
    up_pieces = frozen_pieces(hops, ffn_out_weight, parity)
    shard = jnp.stack(
        [
            jnp.transpose(adapter_down, (1, 0, 2)).reshape(rows, n_adapters * rank),
            adapter_up.reshape(n_adapters * rank, rows).T,
            merging_query,
            merging_key,
            merging_value,
        ]
    )
    weights = lax.all_gather(shard, AXES, axis=1, tiled=True)

    flat, turned, att, prob, first, normed1, inv_std1 = call_attend_forward(
        meta, doc_lengths, tokens, line(norm1_gain), line(norm1_bias), qkv_pieces, out_pieces
    )
    slope, sums = call_ffn_forward(meta, first, in_pieces, up_pieces)
    layer_out, grad_sum2, grad_sum2_low, grads, lines = call_merging(
        n_adapters,
        meta,
        doc_lengths,
        sums,
        line(norm2_gain),
        line(norm2_bias),
        line(merging_gain),
        line(merging_bias),
        out_grad,
        weights,
        F32,
    )
    grad_sum1, grad_sum1_low = call_ffn_backward(
        meta, grad_sum2, grad_sum2_low, normed1, inv_std1, line(norm1_gain), slope, in_pieces, up_pieces
    )
    input_grad = call_attend_backward(
        meta, grad_sum1, grad_sum1_low, flat, turned, att, prob, qkv_pieces, out_pieces
    )
    grads = lax.psum_scatter(grads, AXES, scatter_dimension=1, tiled=True)
    lines = lax.psum(lines, AXES)
    return (
        layer_out,
        input_grad,
        grads[0],
        grads[1],
        grads[2],
        lines[0],
        lines[1],
        lines[2, :n_adapters] / lines[2, n_adapters],
    )


def solution(mesh):
    split = P(AXES, None)
    in_specs = (
        split,
        P("dp", None),
        P(None, "tensor"),
        P("tensor", None),
        P(),
        P(),
        P(None, "tensor"),
        P("tensor", None),
        P(),
        P(),
        P(None, AXES, None),
        P(None, None, AXES),
        split,
        split,
        split,
        P(),
        P(),
        split,
    )
    out_specs = (split, split, split, split, split, P(), P(), P())
    return jax.shard_map(
        functools.partial(per_device, Hops(mesh)),
        mesh=mesh,
        in_specs=in_specs,
        out_specs=out_specs,
        check_vma=False,
    )
```

time: 1190 us -> 288 us (0.24)
  waiting for transfers between devices: 797 us -> 118 us
  matrix products: 170 us -> 0 us
  Pallas kernels: 0 us -> 80 us
  other arithmetic: 77.3 us -> 1.77 us
  local copies, waits for them, and re-layouts: 77.9 us -> 20.7 us
  starting transfers between devices: 0.79 us -> 13.1 us
    reduce_scatter x6 -> x1, waiting for transfers between devices: 412 us -> 45.3 us  [per_device(): grads = lax.psum_scatter(grads, AXES, scatter_dimension=1, tiled=True)]
    all_gather x8 -> x1, waiting for transfers between devices: 254 us -> 0.02 us  [per_device(): weights = lax.all_gather(shard, AXES, axis=1, tiled=True)]
    dot_general x95 -> x0, matrix products: 168 us -> none  [the longest x15 33.1 us: contract_last(): lax.dot_general(left_side, right_side, (((1,), (1,)), ((), ())), preferre...]
    psum x1 -> x0, waiting for transfers between devices: 127 us -> none  [per_device(): lax.psum(jnp.dot(attended_flat, attn_weight, preferred_element_type=jnp.f...]
    pallas_call x0 -> x5, Pallas kernels: none -> 80 us  [the longest x1 19.3 us: call_merging(): pl.pallas_call(functools.partial(merging, n_adapters), in_specs=[SMEM, SM...]
    ppermute x0 -> x20, waiting for transfers between devices: none -> 72.4 us  [flip(): return lax.ppermute(array, AXES, [(i, i ^ bits) for i in range(self.count)])]
    reduce_sum x33 -> x0, other arithmetic: 38.9 us -> none  [the longest x4 11.9 us: mixing_block(): jnp.sum(grad_adapted, axis=1, dtype=jnp.float32)]
    while x345 -> x0, local copies, waits for them, and re-layouts: 20.7 us -> none
  transfers between devices with their start and end apart: 15 -> 22, of which waited for: 14 -> 7; matrix products, arithmetic and copies ran while one was open for 3% -> 4% of each run, Pallas kernels for 0% -> 21%
where the time goes in v1:
time: 288 us
  waiting for transfers between devices  118 us (41%)
  Pallas kernels  80 us (28%)
  blocking collectives  40 us (14%)
  local copies, waits for them, and re-layouts  20.7 us (7%)
  between operations  14.3 us (5%)
  starting transfers between devices  13.1 us (5%)
    ppermute x20, waiting for transfers between devices, flip(): return lax.ppermute(array, AXES, [(i, i ^ bits) for i in range(self.count)])  72.4 us
    reduce_scatter x1, waiting for transfers between devices, per_device(): grads = lax.psum_scatter(grads, AXES, scatter_dimension=1, tiled=True)  45.3 us
    psum x1, blocking collectives, per_device(): lines = lax.psum(lines, AXES)  40 us
    pallas_call x1, Pallas kernels, call_merging(): pl.pallas_call(functools.partial(merging, n_adapters), in_specs=[SMEM, SM...  19.3 us
    pallas_call x1, Pallas kernels, call_attend_backward(): pl.pallas_call(attend_backward, grid=(4,), in_specs=[SMEM, whole((seq, wi...  18.4 us
    pallas_call x1, Pallas kernels, call_attend_forward(): pl.pallas_call(attend_forward, grid=(4,), in_specs=[SMEM, SMEM, whole((se...  17.7 us
    ppermute x20, starting transfers between devices, flip(): return lax.ppermute(array, AXES, [(i, i ^ bits) for i in range(self.count)])  13 us
    pallas_call x1, Pallas kernels, call_ffn_backward(): pl.pallas_call(ffn_backward, grid=(4,), in_specs=[SMEM, whole((seq, width...  13 us
  transfers between devices with their start and end apart: 22, of which 7 were waited for; matrix products, arithmetic and copies ran while one was open for 4% of the time, Pallas kernels for 21%

profile of v1, /device:TPU:0, one launch (start us, length us, event | category | flops | bytes accessed | tf_op | source)
XLA Modules:
  0.0 287.5 jit_solution(12240252315510802990)
XLA Ops:
  12.5 1.6 constant_dynamic-slice_fusion.2
  14.1 2.9 %collective-permute-start.6 = (bf16[96,768]{1,0:T(8,128)(2,1)}, bf16[96,768]{1,0:T(8,128)(2,1)S(1)}, u32[]{:S(2)}, u32[]{:S(2)}) collective-permute-start(bf16[96,768]{1,0:T(8,128)(2,1)} %constant_dynamic-slice_fusion.2), channel_id=1, source_target_pairs={{0,2},{1,3},{2,0},{3,1},{4,6},{5,7},{6,4},{7,5},{8,10},{9,11},{10,... | collective-permute-start | bytes 442376 | tf_op jit(solution)/shard_map/ppermute | solution.py:507
  18.1 1.6 copy.33.refs_5_.refs_7_
  19.8 2.0 collective-permute-done.6.refs_13_.refs_15_
  21.8 2.3 collective-permute-start.1
  25.0 1.5 collective-permute-start.7
  26.6 4.6 %collective-permute-done.7.refs_14_.refs_16_ = bf16[96,768]{1,0:T(8,128)(2,1)S(1)} collective-permute-done((bf16[96,768]{1,0:T(8,128)(2,1)S(1)}, bf16[96,768]{1,0:T(8,128)(2,1)S(1)}, u32[]{:S(2)}, u32[]{:S(2)}) %collective-permute-start.7) | collective-permute-done | bytes 147488 | tf_op jit(solution)/shard_map/ppermute | solution.py:507
  31.1 1.5 collective-permute-start.11
  32.6 17.3 %collective-permute-done.1.refs_7_.refs_9_ = bf16[384,576]{1,0:T(8,128)(2,1)S(1)} collective-permute-done((bf16[384,576]{1,0:T(8,128)(2,1)S(1)}, bf16[384,576]{1,0:T(8,128)(2,1)S(1)}, u32[]{:S(2)}, u32[]{:S(2)}) %collective-permute-start.1) | collective-permute-done | bytes 442400 | tf_op jit(solution)/shard_map/ppermute | solution.py:507
  49.9 1.4 collective-permute-start.2
  51.5 12.2 %collective-permute-done.11.refs_4_.refs_9_ = bf16[384,768]{1,0:T(8,128)(2,1)} collective-permute-done((bf16[384,768]{1,0:T(8,128)(2,1)S(1)}, bf16[384,768]{1,0:T(8,128)(2,1)}, u32[]{:S(2)}, u32[]{:S(2)}) %collective-permute-start.11) | collective-permute-done | bytes 589856 | tf_op jit(solution)/shard_map/ppermute | solution.py:507
  63.6 1.8 collective-permute-start.17
  66.5 24.1 %collective-permute-done.17.refs_11_.refs_16_ = bf16[384,768]{1,0:T(8,128)(2,1)} collective-permute-done((bf16[384,768]{1,0:T(8,128)(2,1)}, bf16[384,768]{1,0:T(8,128)(2,1)}, u32[]{:S(2)}, u32[]{:S(2)}) %collective-permute-start.17) | collective-permute-done | bytes 589856 | tf_op jit(solution)/shard_map/ppermute | solution.py:507
  90.6 12.3 %collective-permute-done.12.refs_5_.refs_10_ = bf16[384,768]{1,0:T(8,128)(2,1)} collective-permute-done((bf16[384,768]{1,0:T(8,128)(2,1)}, bf16[384,768]{1,0:T(8,128)(2,1)}, u32[]{:S(2)}, u32[]{:S(2)}) %collective-permute-start.12) | collective-permute-done | bytes 589856 | tf_op jit(solution)/shard_map/ppermute | solution.py:507
  108.3 2.2 copy.34.refs_6_.refs_8_
  110.6 17.7 %attend_forward.1 = (bf16[4,512,576]{2,1,0:T(8,128)(2,1)}, bf16[4,576,512]{2,1,0:T(8,128)(2,1)}, bf16[4,192,512]{2,1,0:T(8,128)(2,1)}, bf16[4,3,512,512]{3,2,1,0...) custom-call(s32[2]{0:T(128)} %pad_add_fusion.refs_0_.meta, s32[4,8]{1,0:T(4,128)} %lengths.1, ...), custom_call_target="tpu_custom_call" | custom-call | tf_op jit(solution)/shard_map/attend_forward/pallas_call | solution.py:172
  128.4 11.6 %ffn_forward.1 = (bf16[4,512,768]{2,1,0:T(8,128)(2,1)}, f32[512,768]{1,0:T(8,128)}) custom-call(s32[2]{0:T(128)} %pad_add_fusion.refs_0_.meta, f32[512,768]{1,0:T(8,128)} %get-tuple-element.24.refs_1_, bf16[768,768]{1,0:T(8,128)(2,1)} %refs_7_.2, bf16[768,768]{1,0:T(8,128)(2,1)} %collective-permute-done.10.refs_3_.refs_8_, ...), custom_call_target="tpu_custom_call" | custom-call | tf_op jit(solution)/shard_map/ffn_forward/pallas_call | solution.py:234
  140.1 19.3 %merging.1 = (f32[512,768]{1,0:T(8,128)}, f32[512,768]{1,0:T(8,128)}, bf16[512,768]{1,0:T(8,128)(2,1)}, f32[3,768,768]{2,1,0:T(8,128)}, f32[8,768]{1,0:T(8,128)}) custom-call(s32[2]{0:T(128)} %pad_add_fusion.refs_0_.meta, s32[4,8]{1,0:T(4,128)} %lengths.1, f32[512,768]{1,0:T(8,128)} %get-tuple-element.25.sums, f32[1,768]{1,0:T(1,128)} %broadcast_in_dim.21.gain2, ...), custom_call_target="tpu_custom_call" | custom-call | tf_op jit(solution)/shard_map/merging/pallas_call | solution.py:353
  160.1 40.0 %psum.7 = f32[8,768]{1,0:T(8,128)S(1)} all-reduce(f32[8,768]{1,0:T(8,128)S(1)} %copy-done.12), channel_id=1, replica_groups=mesh['dp'=8,'tensor'=4] {'dp','tensor'}, use_global_device_ids=true, to_apply=%region_1.2 | all-reduce | flops 6144 | bytes 49152 | tf_op jit(solution)/shard_map/psum | solution.py:584
  200.6 13.0 %ffn_backward.1 = (f32[512,768]{1,0:T(8,128)}, bf16[512,768]{1,0:T(8,128)(2,1)}) custom-call(s32[2]{0:T(128)} %pad_add_fusion.refs_0_.meta, f32[512,768]{1,0:T(8,128)} %get-tuple-element.27.refs_1_, bf16[512,768]{1,0:T(8,128)(2,1)} %get-tuple-element.28.refs_2_, f32[512,768]{1,0:T(8,128)} %get-tuple-element.29.refs_3_, f32[512,1]{1,0:T(8,128)} %get-tuple-element.30.refs_4_, ...), custom_call_target="tpu_custom_call" | custom-call | tf_op jit(solution)/shard_map/ffn_backward/pallas_call | solution.py:401
  213.6 18.4 %attend_backward.1 = f32[512,768]{1,0:T(8,128)} custom-call(s32[2]{0:T(128)} %pad_add_fusion.refs_0_.meta, f32[512,768]{1,0:T(8,128)} %get-tuple-element.32.refs_1_, bf16[512,768]{1,0:T(8,128)(2,1)} %get-tuple-element.33.refs_2_, bf16[4,512,576]{2,1,0:T(8,128)(2,1)} %get-tuple-element.34.refs_3_, bf16[4,576,512]{2,1,0:T(8,128)(2,1)} %get-tuple-element.35.refs_4_, ...), custom_call_target="tpu_custom_call" | custom-call | tf_op jit(solution)/shard_map/attend_backward/pallas_call | solution.py:473
  232.6 1.2 fusion
  233.7 45.3 %reduce-scatter.2.cloned.1.call-done = f32[3,24,768]{2,1,0:T(8,128)} async-done(((f32[3,768,768]{2,1,0:T(8,128)}), f32[3,24,768]{2,1,0:T(8,128)}) %reduce-scatter.2.cloned.1.call-update) | async-done | bytes 221200 | tf_op jit(solution)/shard_map/reduce_scatter | solution.py:583
  279.0 1.6 slice_bitcast_fusion
  (92 shorter events, 16.0 us)
Async XLA Ops:
  7.2 132.9 %all-gather.2.cloned.1.call-start = ((), (), s32[]{:S(2)}) async-start(), calls=%async_computation.1 | async-start | bytes 6082560 | tf_op jit(solution)/shard_map/all_gather | solution.py:558
  12.5 266.6 %reduce-scatter.2.cloned.1.call-start = ((), (), s32[]{:S(2)}) async-start(), calls=%async_computation.2 | async-start | bytes 7299072 | tf_op jit(solution)/shard_map/reduce_scatter | solution.py:583
  14.1 7.7 %collective-permute-start.6 = (bf16[96,768]{1,0:T(8,128)(2,1)}, bf16[96,768]{1,0:T(8,128)(2,1)S(1)}, u32[]{:S(2)}, u32[]{:S(2)}) collective-permute-start(bf16[96,768]{1,0:T(8,128)(2,1)} %constant_dynamic-slice_fusion.2), channel_id=1, source_target_pairs={{0,2},{1,3},{2,0},{3,1},{4,6},{5,7},{6,4},{7,5},{8,10},{9,11},{10,... | collective-permute-start | bytes 442376 | tf_op jit(solution)/shard_map/ppermute | solution.py:507
  17.9 89.2 %copy-start.18 = (f32[768]{0:T(1024)S(1)}, f32[768]{0:T(1024)}, u32[]{:S(2)}) copy-start(f32[768]{0:T(1024)} %param.34) | copy-start | bytes 9220
  18.0 33.3 %collective-permute-start.16 = (bf16[384,768]{1,0:T(8,128)(2,1)}, bf16[384,768]{1,0:T(8,128)(2,1)}, u32[]{:S(2)}, u32[]{:S(2)}) collective-permute-start(bf16[384,768]{1,0:T(8,128)(2,1)} %constant_dynamic-slice_fusion), channel_id=1, source_target_pairs={{0,2},{1,3},{2,0},{3,1},{4,6},{5,7},{6,4},{7,5},{8,10},{9,11},{10,... | collective-permute-start | bytes 1769480 | tf_op jit(solution)/shard_map/ppermute | solution.py:507
  18.0 45.6 %collective-permute-start = (bf16[768,576]{0,1:T(8,128)(2,1)}, bf16[768,576]{0,1:T(8,128)(2,1)}, u32[]{:S(2)}, u32[]{:S(2)}) collective-permute-start(bf16[768,576]{0,1:T(8,128)(2,1)} %param.20), channel_id=1, source_target_pairs={{0,1},{1,0},{2,3},{3,2},{4,5},{5,4},{6,7},{7,6},{8,9},{9,8},{10,11... | collective-permute-start | bytes 2654216 | tf_op jit(solution)/shard_map/ppermute | solution.py:507
  19.8 90.8 %copy-start = (bf16[768,576]{1,0:T(8,128)(2,1)}, bf16[768,576]{1,0:T(8,128)(2,1)S(1)}, u32[]{:S(2)}) copy-start(bf16[768,576]{1,0:T(8,128)(2,1)S(1)} %copy.33.refs_5_.refs_7_) | copy-start | bytes 2654212
  21.8 2.6 collective-permute-start.8
  21.8 28.1 %collective-permute-start.1 = (bf16[384,576]{1,0:T(8,128)(2,1)S(1)}, bf16[384,576]{1,0:T(8,128)(2,1)S(1)}, u32[]{:S(2)}, u32[]{:S(2)}) collective-permute-start(bf16[384,576]{1,0:T(8,128)(2,1)S(1)} %constant_dynamic-slice_fusion.3), channel_id=1, source_target_pairs={{0,2},{1,3},{2,0},{3,1},{4,6},{5,7},{6,4},{7,5},{8,10},{9,11},{10,... | collective-permute-start | bytes 1327112 | tf_op jit(solution)/shard_map/ppermute | solution.py:507
  24.1 8.5 %collective-permute-start.5 = (bf16[192,768]{1,0:T(8,128)(2,1)}, bf16[192,768]{1,0:T(8,128)(2,1)S(1)}, u32[]{:S(2)}, u32[]{:S(2)}) collective-permute-start(bf16[192,768]{1,0:T(8,128)(2,1)} %refs_13_.3), channel_id=1, source_target_pairs={{0,1},{1,0},{2,3},{3,2},{4,5},{5,4},{6,7},{7,6},{8,9},{9,8},{10,11... | collective-permute-start | bytes 884744 | tf_op jit(solution)/shard_map/ppermute | solution.py:507
  25.0 6.1 %collective-permute-start.7 = (bf16[96,768]{1,0:T(8,128)(2,1)S(1)}, bf16[96,768]{1,0:T(8,128)(2,1)S(1)}, u32[]{:S(2)}, u32[]{:S(2)}) collective-permute-start(bf16[96,768]{1,0:T(8,128)(2,1)S(1)} %collective-permute-done.6.refs_13_.refs_15_), channel_id=1, source_target_pairs={{0,4},{1,5},{2,6},{3,7},{4,0},{5,1},{6,2},{7,3},{8,12},{9,13},{10,... | collective-permute-start | bytes 442376 | tf_op jit(solution)/shard_map/ppermute | solution.py:507
  31.1 32.5 %collective-permute-start.11 = (bf16[384,768]{1,0:T(8,128)(2,1)S(1)}, bf16[384,768]{1,0:T(8,128)(2,1)}, u32[]{:S(2)}, u32[]{:S(2)}) collective-permute-start(bf16[384,768]{1,0:T(8,128)(2,1)S(1)} %constant_dynamic-slice_fusion.1), channel_id=1, source_target_pairs={{0,2},{1,3},{2,0},{3,1},{4,6},{5,7},{6,4},{7,5},{8,10},{9,11},{10,... | collective-permute-start | bytes 1769480 | tf_op jit(solution)/shard_map/ppermute | solution.py:507
  32.6 17.3 %collective-permute-start.9 = (bf16[96,768]{1,0:T(8,128)(2,1)S(1)}, bf16[96,768]{1,0:T(8,128)(2,1)}, u32[]{:S(2)}, u32[]{:S(2)}) collective-permute-start(bf16[96,768]{1,0:T(8,128)(2,1)S(1)} %collective-permute-done.7.refs_14_.refs_16_), channel_id=1, source_target_pairs={{0,1},{1,0},{2,3},{3,2},{4,5},{5,4},{6,7},{7,6},{8,9},{9,8},{10,11... | collective-permute-start | bytes 442376 | tf_op jit(solution)/shard_map/ppermute | solution.py:507
  49.9 15.5 %collective-permute-start.3 = (bf16[384,576]{1,0:T(8,128)(2,1)S(1)}, bf16[384,576]{1,0:T(8,128)(2,1)S(1)}, u32[]{:S(2)}, u32[]{:S(2)}) collective-permute-start(bf16[384,576]{1,0:T(8,128)(2,1)S(1)} %collective-permute-done.1.refs_7_.refs_9_), channel_id=1, source_target_pairs={{0,1},{1,0},{2,3},{3,2},{4,5},{5,4},{6,7},{7,6},{8,9},{9,8},{10,11... | collective-permute-start | bytes 1327112 | tf_op jit(solution)/shard_map/ppermute | solution.py:507
  49.9 15.8 %collective-permute-start.2 = (bf16[384,576]{1,0:T(8,128)(2,1)S(1)}, bf16[384,576]{1,0:T(8,128)(2,1)S(1)}, u32[]{:S(2)}, u32[]{:S(2)}) collective-permute-start(bf16[384,576]{1,0:T(8,128)(2,1)S(1)} %collective-permute-done.1.refs_7_.refs_9_), channel_id=1, source_target_pairs={{0,4},{1,5},{2,6},{3,7},{4,0},{5,1},{6,2},{7,3},{8,12},{9,13},{10,... | collective-permute-start | bytes 1327112 | tf_op jit(solution)/shard_map/ppermute | solution.py:507
  51.3 14.4 %collective-permute-start.18 = (bf16[384,768]{1,0:T(8,128)(2,1)}, bf16[384,768]{1,0:T(8,128)(2,1)}, u32[]{:S(2)}, u32[]{:S(2)}) collective-permute-start(bf16[384,768]{1,0:T(8,128)(2,1)} %collective-permute-done.16.refs_10_.refs_15_), channel_id=1, source_target_pairs={{0,1},{1,0},{2,3},{3,2},{4,5},{5,4},{6,7},{7,6},{8,9},{9,8},{10,11... | collective-permute-start | bytes 1769480 | tf_op jit(solution)/shard_map/ppermute | solution.py:507
  63.6 64.7 %collective-permute-start.10 = (bf16[768,768]{1,0:T(8,128)(2,1)S(1)}, bf16[768,768]{1,0:T(8,128)(2,1)}, u32[]{:S(2)}, u32[]{:S(2)}) collective-permute-start(bf16[768,768]{1,0:T(8,128)(2,1)S(1)} %copy-done.1), channel_id=1, source_target_pairs={{0,1},{1,0},{2,3},{3,2},{4,5},{5,4},{6,7},{7,6},{8,9},{9,8},{10,11... | collective-permute-start | bytes 3538952 | tf_op jit(solution)/shard_map/ppermute | solution.py:507
  63.6 27.0 %collective-permute-start.17 = (bf16[384,768]{1,0:T(8,128)(2,1)}, bf16[384,768]{1,0:T(8,128)(2,1)}, u32[]{:S(2)}, u32[]{:S(2)}) collective-permute-start(bf16[384,768]{1,0:T(8,128)(2,1)} %collective-permute-done.16.refs_10_.refs_15_), channel_id=1, source_target_pairs={{0,4},{1,5},{2,6},{3,7},{4,0},{5,1},{6,2},{7,3},{8,12},{9,13},{10,... | collective-permute-start | bytes 1769480 | tf_op jit(solution)/shard_map/ppermute | solution.py:507
  65.4 37.5 %collective-permute-start.12 = (bf16[384,768]{1,0:T(8,128)(2,1)}, bf16[384,768]{1,0:T(8,128)(2,1)}, u32[]{:S(2)}, u32[]{:S(2)}) collective-permute-start(bf16[384,768]{1,0:T(8,128)(2,1)} %collective-permute-done.11.refs_4_.refs_9_), channel_id=1, source_target_pairs={{0,4},{1,5},{2,6},{3,7},{4,0},{5,1},{6,2},{7,3},{8,12},{9,13},{10,... | collective-permute-start | bytes 1769480 | tf_op jit(solution)/shard_map/ppermute | solution.py:507
  65.7 62.7 %collective-permute-start.15 = (bf16[768,768]{1,0:T(8,128)(2,1)S(1)}, bf16[768,768]{1,0:T(8,128)(2,1)}, u32[]{:S(2)}, u32[]{:S(2)}) collective-permute-start(bf16[768,768]{1,0:T(8,128)(2,1)S(1)} %copy-done.2), channel_id=1, source_target_pairs={{0,1},{1,0},{2,3},{3,2},{4,5},{5,4},{6,7},{7,6},{8,9},{9,8},{10,11... | collective-permute-start | bytes 3538952 | tf_op jit(solution)/shard_map/ppermute | solution.py:507
  66.2 36.7 %collective-permute-start.4 = (bf16[384,576]{1,0:T(8,128)(2,1)S(1)}, bf16[384,576]{1,0:T(8,128)(2,1)S(1)}, u32[]{:S(2)}, u32[]{:S(2)}) collective-permute-start(bf16[384,576]{1,0:T(8,128)(2,1)S(1)} %collective-permute-done.2.refs_8_.refs_10_), channel_id=1, source_target_pairs={{0,1},{1,0},{2,3},{3,2},{4,5},{5,4},{6,7},{7,6},{8,9},{9,8},{10,11... | collective-permute-start | bytes 1327112 | tf_op jit(solution)/shard_map/ppermute | solution.py:507
  90.6 37.7 %collective-permute-start.13 = (bf16[384,768]{1,0:T(8,128)(2,1)}, bf16[384,768]{1,0:T(8,128)(2,1)}, u32[]{:S(2)}, u32[]{:S(2)}) collective-permute-start(bf16[384,768]{1,0:T(8,128)(2,1)} %collective-permute-done.11.refs_4_.refs_9_), channel_id=1, source_target_pairs={{0,1},{1,0},{2,3},{3,2},{4,5},{5,4},{6,7},{7,6},{8,9},{9,8},{10,11... | collective-permute-start | bytes 1769480 | tf_op jit(solution)/shard_map/ppermute | solution.py:507
  102.9 25.5 %collective-permute-start.19 = (bf16[384,768]{1,0:T(8,128)(2,1)}, bf16[384,768]{1,0:T(8,128)(2,1)}, u32[]{:S(2)}, u32[]{:S(2)}) collective-permute-start(bf16[384,768]{1,0:T(8,128)(2,1)} %collective-permute-done.17.refs_11_.refs_16_), channel_id=1, source_target_pairs={{0,1},{1,0},{2,3},{3,2},{4,5},{5,4},{6,7},{7,6},{8,9},{9,8},{10,11... | collective-permute-start | bytes 1769480 | tf_op jit(solution)/shard_map/ppermute | solution.py:507
  103.7 24.7 %collective-permute-start.14 = (bf16[384,768]{1,0:T(8,128)(2,1)}, bf16[384,768]{1,0:T(8,128)(2,1)}, u32[]{:S(2)}, u32[]{:S(2)}) collective-permute-start(bf16[384,768]{1,0:T(8,128)(2,1)} %collective-permute-done.12.refs_5_.refs_10_), channel_id=1, source_target_pairs={{0,1},{1,0},{2,3},{3,2},{4,5},{5,4},{6,7},{7,6},{8,9},{9,8},{10,11... | collective-permute-start | bytes 1769480 | tf_op jit(solution)/shard_map/ppermute | solution.py:507
  (17 other events, 707.0 us)
Sparse Core Ops, SparseCore 0:
  12.6 86.4 all-gather.1
  159.5 119.5 reduce-scatter.1

commit v2 on v1

--- a/solution.py
+++ b/solution.py
@@ -17,9 +17,16 @@
 ROOT_TAU = 0.3989422804014327
 F32, BF16 = jnp.float32, jnp.bfloat16
 
+CORE, ACROSS, PAIR_Y, PAIR_Z, DEPTH, ROW = range(6)
+GAIN1, SHIFT1, GAIN2, SHIFT2, GAIN3, SHIFT3 = range(6)
+
 SMEM = pl.BlockSpec(memory_space=pltpu.SMEM)
 VMEM = pl.BlockSpec(memory_space=pltpu.VMEM)
 ANY = pl.BlockSpec(memory_space=pl.ANY)
+
+
+def line_of(lines, i):
+    return lines[i : i + 1]
 
 
 def dot(a, b):
@@ -89,7 +96,7 @@
 
 def segment_bias(meta_ref, lengths_ref, bias_ref):
     seq = bias_ref.shape[0]
-    row = meta_ref[1]
+    row = meta_ref[ROW]
     by_row = lax.broadcasted_iota(jnp.int32, (seq, 1), 0)
     by_lane = lax.broadcasted_iota(jnp.int32, (1, seq), 1)
     seg_row = jnp.zeros((seq, 1), jnp.int32)
@@ -102,33 +109,25 @@
     bias_ref[...] = jnp.where(seg_row == seg_lane, 0.0, BIG_NEGATIVE).astype(F32)
 
 
-def attend_forward(*refs):
-    meta, lengths, tokens, gain, shift = refs[:5]
-    qkv_pieces, out_pieces = refs[5 : 5 + N_PIECES], refs[5 + N_PIECES : 5 + 2 * N_PIECES]
-    rest = refs[5 + 2 * N_PIECES :]
+def attend_forward(columns, *refs):
+    meta, lengths, tokens, lines = refs[:4]
+    pieces, rest = refs[4 : 4 + N_PIECES], refs[4 + N_PIECES :]
     flat_out, turned_out, att_out, prob_out, first_out, normed_out, inv_out = rest[:7]
-    qkv_w, out_w, bias, total, sems, out_sems = rest[7:]
+    weight, bias, total, sems = rest[7:]
     step = pl.program_id(0)
-    parity = meta[0]
-    bring_quarters(
-        step,
-        (
-            piece_copies(qkv_pieces, PLACE, parity, qkv_w, sems),
-            piece_copies(out_pieces, PLACE, parity, out_w, out_sems),
-        ),
-    )
+    bring_quarters(step, (piece_copies(pieces, PLACE, meta[PAIR_Y], weight, sems),))
 
     @pl.when(step == 0)
     def _():
         segment_bias(meta, lengths, bias)
         total[...] = tokens[...].astype(F32)
 
-    flat = dot(tokens[...], qkv_w[step]).astype(BF16)
+    turned = dot_last(weight[step, :columns], tokens[...]).astype(BF16)
+    turned_out[0] = turned
+    flat = turned.T
     flat_out[0] = flat
-    turned = flat.T
-    turned_out[0] = turned
     width = 3 * HEAD_DIM
-    for head in range(flat.shape[1] // width):
+    for head in range(columns // width):
         base = head * width
         keys = flat[:, base + HEAD_DIM : base + 2 * HEAD_DIM]
         queries = turned[base : base + HEAD_DIM] * BF16(HEAD_DIM**-0.5)
@@ -138,14 +137,14 @@
         prob = (exponent * (1.0 / jnp.sum(exponent, axis=0, keepdims=True))).astype(BF16)
         prob_out[0, head] = prob
         att_out[0, head * HEAD_DIM : (head + 1) * HEAD_DIM] = dot(values, prob).astype(BF16)
-    total[...] += dot(att_out[0].T, out_w[step])
+    total[...] += dot(att_out[0].T, weight[step, columns:])
 
     @pl.when(step == 3)
     def _():
         normed, inv_std = normalize(total[...])
         normed_out[...] = normed
         inv_out[...] = inv_std
-        first_out[...] = normed * gain[...] + shift[...]
+        first_out[...] = normed * line_of(lines, GAIN1) + line_of(lines, SHIFT1)
 
 
 def whole(shape):
@@ -164,16 +163,19 @@
     return pltpu.CompilerParams(vmem_limit_bytes=VMEM_BYTES, **kw)
 
 
-def call_attend_forward(meta, lengths, tokens, gain, shift, qkv_pieces, out_pieces):
+def cost(us):
+    return pl.CostEstimate(flops=int(us * 1.1e9), bytes_accessed=1 << 20, transcendentals=0)
+
+
+def call_attend_forward(columns, meta, lengths, tokens, lines, pieces):
     seq, width = tokens.shape
-    columns = qkv_pieces[0].shape[1]
+    rows = pieces[0].shape[0]
     heads = columns // (3 * HEAD_DIM)
     inner = heads * HEAD_DIM
     return pl.pallas_call(
-        attend_forward,
+        functools.partial(attend_forward, columns),
         grid=(4,),
-        in_specs=[SMEM, SMEM, whole((seq, width)), whole((1, width)), whole((1, width))]
-        + [ANY] * (2 * N_PIECES),
+        in_specs=[SMEM, SMEM, whole((seq, width)), whole(lines.shape)] + [ANY] * N_PIECES,
         out_specs=[
             by_quarter((seq, columns)),
             by_quarter((columns, seq)),
@@ -193,16 +195,15 @@
             sds((seq, 1), F32),
         ],
         scratch_shapes=[
-            pltpu.VMEM((4, width, columns), BF16),
-            pltpu.VMEM((4, inner, width), BF16),
+            pltpu.VMEM((4, rows, width), BF16),
             pltpu.VMEM((seq, seq), F32),
             pltpu.VMEM((seq, width), F32),
             pltpu.SemaphoreType.DMA((N_PIECES,)),
-            pltpu.SemaphoreType.DMA((N_PIECES,)),
         ],
         compiler_params=params(),
+        cost_estimate=cost(16),
         name="attend_forward",
-    )(meta, lengths, tokens, gain, shift, *qkv_pieces, *out_pieces)
+    )(meta, lengths, tokens, lines, *pieces)
 
 
 def ffn_forward(*refs):
@@ -213,8 +214,8 @@
     bring_quarters(
         step,
         (
-            piece_copies(in_pieces, PLACE, meta[0], in_w, sems),
-            piece_copies(out_pieces, PLACE, meta[0], out_w, out_sems),
+            piece_copies(in_pieces, PLACE, meta[PAIR_Z], in_w, sems),
+            piece_copies(out_pieces, PLACE, meta[PAIR_Z], out_w, out_sems),
         ),
     )
 
@@ -245,30 +246,54 @@
             pltpu.SemaphoreType.DMA((N_PIECES,)),
         ],
         compiler_params=params(),
+        cost_estimate=cost(11),
         name="ffn_forward",
     )(meta, first, *in_pieces, *out_pieces)
 
 
-def merging(
-    n_adapters,
-    meta,
-    lengths,
-    sums,
-    gain2,
-    shift2,
-    gain3,
-    shift3,
-    out_grad,
-    weights,
-    layer_out,
-    grad_sum2_out,
-    grad_low_out,
-    grad_out,
-    lines_out,
-):
+def tile_copies(meta, tiles, weights, sems):
+    n_mats, width, _ = weights.shape
+    half = width // 2
+    copies = []
+    for y_rel in range(2):
+        for z_rel in range(4):
+            for core_rel in range(2):
+                tile = tiles[(y_rel * 4 + z_rel) * 2 + core_rel]
+                rows = tile.shape[1]
+                side = pl.multiple_of((meta[CORE] ^ core_rel) * half, LANES)
+                for x_rel in range(2):
+                    chip = ((meta[DEPTH] ^ z_rel) * 2 + (meta[PAIR_Y] ^ y_rel)) * 2
+                    chip = chip + (meta[ACROSS] ^ x_rel)
+                    target = weights.at[
+                        :, pl.ds(pl.multiple_of(chip * rows, 16), rows), pl.ds(side, half)
+                    ]
+                    source = tile.at[pl.ds(x_rel * n_mats, n_mats)]
+                    copies.append(pltpu.make_async_copy(source, target, sems.at[len(copies)]))
+    return copies
+
+
+def split_lines(total):
+    high = total.astype(BF16).astype(F32)
+    return jnp.concatenate([high, total - high], axis=0)
+
+
+def merging(n_adapters, tiled, meta, lengths, sums, lines, out_grad, *refs):
+    n_tiles = 16 if tiled else 1
+    tiles, refs = refs[:n_tiles], refs[n_tiles:]
+    layer_out, grad_sum2_out, grad_low_out = refs[:3]
+    if tiled:
+        keep_out, send_out, weights, grads, sems = refs[3:]
+        copies = tile_copies(meta, tiles, weights, sems)
+        for copy in copies:
+            copy.start()
+    else:
+        grads, lines_out = refs[3:]
+        weights = tiles[0]
     seq, width = sums.shape
     scale = width**-0.5
     down, up, query, key, value = (weights.at[i] for i in range(5))
+    gain2, shift2 = line_of(lines, GAIN2), line_of(lines, SHIFT2)
+    gain3, shift3 = line_of(lines, GAIN3), line_of(lines, SHIFT3)
     spread = jnp.where(
         lax.broadcasted_iota(jnp.int32, (LANES, width), 0)
         == lax.broadcasted_iota(jnp.int32, (LANES, width), 1) // (width // n_adapters),
@@ -283,8 +308,11 @@
         return dot_last(high, spread) + dot_last(rest, spread)
 
     normed2, inv_std2 = normalize(sums[...])
-    second = normed2 * gain2[...] + shift2[...]
+    second = normed2 * gain2 + shift2
     second_low = second.astype(BF16)
+    if tiled:
+        for copy in copies:
+            copy.wait()
     middle = dot(second_low, down[...])
     act, slope = gelu_both(middle)
     act = act.astype(BF16).astype(F32)
@@ -302,23 +330,29 @@
     mix_wide = dot(mix_low, spread)
     blended = (second * mix_sum + dot_last((mix_wide * act).astype(BF16), up[...])).astype(BF16)
     normed3, inv_std3 = normalize(second + dot(blended, value[...]))
-    layer_out[...] = normed3 * gain3[...] + shift3[...]
+    layer_out[...] = normed3 * gain3 + shift3
 
     count = jnp.int32(0)
     for i in range(lengths.shape[1]):
-        count = count + lengths[meta[1], i]
+        count = count + lengths[meta[ROW], i]
     keep = jnp.where(lax.broadcasted_iota(jnp.int32, (seq, 1), 0) < count, 1.0, 0.0)
     cot = out_grad[...].astype(F32) * keep
-    lines_out[...] = jnp.zeros_like(lines_out)
-    lines_out[0:1] = jnp.sum(cot * normed3, axis=0, keepdims=True)
-    lines_out[1:2] = jnp.sum(cot, axis=0, keepdims=True)
     mass = jnp.sum(mix * keep, axis=0, keepdims=True)
     lane = lax.broadcasted_iota(jnp.int32, (1, LANES), 1)
-    lines_out[2:3, :LANES] = jnp.where(lane == n_adapters, jnp.sum(keep), mass)
-
-    grad_pre = norm_back(cot * gain3[...], normed3, inv_std3)
+    mass = jnp.where(lane == n_adapters, jnp.sum(keep), mass)
+    sum_lines = jnp.concatenate(
+        [
+            jnp.sum(cot * normed3, axis=0, keepdims=True),
+            jnp.sum(cot, axis=0, keepdims=True),
+            jnp.concatenate([mass, jnp.zeros((1, width - LANES), F32)], axis=1),
+            jnp.zeros((1, width), F32),
+        ],
+        axis=0,
+    )
+
+    grad_pre = norm_back(cot * gain3, normed3, inv_std3)
     grad_proj = grad_pre.astype(BF16)
-    grad_out[2] = dot_first(blended, grad_proj).astype(grad_out.dtype)
+    grads[2] = dot_first(blended, grad_proj)
     grad_blend = dot_last(grad_proj, value[...]).astype(BF16)
     blend_up = dot(grad_blend, up[...])
     grad_mix = jnp.sum(grad_blend.astype(F32) * second, axis=1, keepdims=True) + by_adapter(
@@ -330,9 +364,9 @@
     grad_probe = (
         scale * (second * logit_sum + dot_last((logit_wide * act).astype(BF16), up[...]))
     ).astype(BF16)
-    grad_out[1] = dot_first(grad_probe, fquery).astype(grad_out.dtype)
+    grads[1] = dot_first(grad_probe, fquery)
     grad_fquery = dot(grad_probe, key[...]).astype(BF16)
-    grad_out[0] = dot_first(second_low, grad_fquery).astype(grad_out.dtype)
+    grads[0] = dot_first(second_low, grad_fquery)
     grad_middle = ((mix_wide * blend_up + (scale * logit_wide) * probe_up) * slope).astype(BF16)
     grad_second = (
         grad_pre
@@ -341,41 +375,63 @@
         + probe.astype(F32) * (scale * logit_sum)
         + dot_last(grad_middle, down[...])
     )
-    grad_sum2 = norm_back(grad_second * gain2[...], normed2, inv_std2)
+    grad_sum2 = norm_back(grad_second * gain2, normed2, inv_std2)
     grad_sum2_out[...] = grad_sum2
     grad_low_out[...] = grad_sum2.astype(BF16)
 
-
-def call_merging(
-    n_adapters, meta, lengths, sums, gain2, shift2, gain3, shift3, out_grad, weights, grad_type
-):
+    if not tiled:
+        lines_out[...] = jnp.concatenate([sum_lines, jnp.zeros_like(sum_lines)], axis=0)
+        return
+    tail = split_lines(sum_lines)
+    rows = width // 32
+
+    @pl.loop(0, 16)
+    def _(chip):
+        z_rel = (chip // 4) ^ meta[DEPTH]
+        y_rel = (chip // 2 % 2) ^ meta[PAIR_Y]
+        x_rel = (chip % 2) ^ meta[ACROSS]
+        for core_rel, out in ((0, keep_out), (1, send_out)):
+            first = pl.multiple_of((chip * 2 + (meta[CORE] ^ core_rel)) * rows, 8)
+            block = [grads[i, pl.ds(first, rows)] for i in range(3)] + [tail]
+            out[x_rel, y_rel, z_rel] = jnp.concatenate(block, axis=0).astype(BF16)
+
+
+def call_merging(n_adapters, tiled, meta, lengths, sums, lines, out_grad, tiles):
     seq, width = sums.shape
+    block = 3 * width // 32 + 8
+    if tiled:
+        out_shape = [sds((2, 2, 4, block, width), BF16)] * 2
+        scratch = [
+            pltpu.VMEM((5, width, width), BF16),
+            pltpu.VMEM((3, width, width), F32),
+            pltpu.SemaphoreType.DMA((32,)),
+        ]
+    else:
+        out_shape = [sds((3, width, width), F32), sds((8, width), F32)]
+        scratch = []
     return pl.pallas_call(
-        functools.partial(merging, n_adapters),
-        in_specs=[SMEM, SMEM] + [VMEM] * 7,
+        functools.partial(merging, n_adapters, tiled),
+        in_specs=[SMEM, SMEM] + [VMEM] * 3 + [ANY if tiled else VMEM] * len(tiles),
         out_specs=[VMEM] * 5,
-        out_shape=[
-            sds((seq, width), F32),
-            sds((seq, width), F32),
-            sds((seq, width), BF16),
-            sds((3, width, width), grad_type),
-            sds((8, width), F32),
-        ],
+        out_shape=[sds((seq, width), F32), sds((seq, width), F32), sds((seq, width), BF16)]
+        + out_shape,
+        scratch_shapes=scratch,
         compiler_params=params(),
+        cost_estimate=cost(18),
         name="merging",
-    )(meta, lengths, sums, gain2, shift2, gain3, shift3, out_grad, weights)
+    )(meta, lengths, sums, lines, out_grad, *tiles)
 
 
 def ffn_backward(*refs):
-    meta, grad_sum2, grad_low, normed1, inv_std1, gain1, slope = refs[:7]
+    meta, grad_sum2, grad_low, normed1, inv_std1, lines, slope = refs[:7]
     in_pieces, out_pieces = refs[7 : 7 + N_PIECES], refs[7 + N_PIECES : 7 + 2 * N_PIECES]
     grad_out, grad_low_out, in_w, out_w, total, sems, out_sems = refs[7 + 2 * N_PIECES :]
     step = pl.program_id(0)
     bring_quarters(
         step,
         (
-            piece_copies(out_pieces, PLACE, meta[0], out_w, out_sems),
-            piece_copies(in_pieces, PLACE, meta[0], in_w, sems),
+            piece_copies(out_pieces, PLACE, meta[PAIR_Z], out_w, out_sems),
+            piece_copies(in_pieces, PLACE, meta[PAIR_Z], in_w, sems),
         ),
     )
 
@@ -388,13 +444,13 @@
 
     @pl.when(step == 3)
     def _():
-        grad = norm_back(total[...] * gain1[...], normed1[...], inv_std1[...])
+        grad = norm_back(total[...] * line_of(lines, GAIN1), normed1[...], inv_std1[...])
         grad_out[...] = grad
         grad_low_out[...] = grad.astype(BF16)
 
 
 def call_ffn_backward(
-    meta, grad_sum2, grad_low, normed1, inv_std1, gain1, slope, in_pieces, out_pieces
+    meta, grad_sum2, grad_low, normed1, inv_std1, lines, slope, in_pieces, out_pieces
 ):
     seq, width = grad_sum2.shape
     hidden = in_pieces[0].shape[1]
@@ -407,7 +463,7 @@
             whole((seq, width)),
             whole((seq, width)),
             whole((seq, 1)),
-            whole((1, width)),
+            whole(lines.shape),
             by_quarter((seq, hidden)),
         ]
         + [ANY] * (2 * N_PIECES),
@@ -421,28 +477,23 @@
             pltpu.SemaphoreType.DMA((N_PIECES,)),
         ],
         compiler_params=params(),
+        cost_estimate=cost(12),
         name="ffn_backward",
-    )(meta, grad_sum2, grad_low, normed1, inv_std1, gain1, slope, *in_pieces, *out_pieces)
-
-
-def attend_backward(*refs):
+    )(meta, grad_sum2, grad_low, normed1, inv_std1, lines, slope, *in_pieces, *out_pieces)
+
+
+def attend_backward(columns, *refs):
     meta, grad_sum1, grad_low, flat_ref, turned_ref, att_ref, prob_ref = refs[:7]
-    qkv_pieces, out_pieces = refs[7 : 7 + N_PIECES], refs[7 + N_PIECES : 7 + 2 * N_PIECES]
-    input_grad, qkv_w, out_w, grad_turned, sems, out_sems = refs[7 + 2 * N_PIECES :]
+    pieces = refs[7 : 7 + N_PIECES]
+    input_grad, weight, grad_turned, sems = refs[7 + N_PIECES :]
     step = pl.program_id(0)
-    bring_quarters(
-        step,
-        (
-            piece_copies(out_pieces, PLACE, meta[0], out_w, out_sems),
-            piece_copies(qkv_pieces, PLACE, meta[0], qkv_w, sems),
-        ),
-    )
+    bring_quarters(step, (piece_copies(pieces, PLACE, meta[PAIR_Y], weight, sems),))
 
     @pl.when(step == 0)
     def _():
         input_grad[...] = grad_sum1[...]
 
-    grad_att = dot_last(out_w[step], grad_low[...]).astype(BF16)
+    grad_att = dot_last(weight[step, columns:], grad_low[...]).astype(BF16)
     width = 3 * HEAD_DIM
     root = HEAD_DIM**-0.5
     for head in range(att_ref.shape[1] // HEAD_DIM):
@@ -460,18 +511,16 @@
             dot_last(queries, grad_scores) * root
         ).astype(BF16)
         grad_turned[base + 2 * HEAD_DIM : base + width] = dot_last(grad, prob).astype(BF16)
-    input_grad[...] += dot_last(grad_turned[...].T, qkv_w[step])
-
-
-def call_attend_backward(
-    meta, grad_sum1, grad_low, flat, turned, att, prob, qkv_pieces, out_pieces
-):
+    input_grad[...] += dot(grad_turned[...].T, weight[step, :columns])
+
+
+def call_attend_backward(columns, meta, grad_sum1, grad_low, flat, turned, att, prob, pieces):
     seq, width = grad_sum1.shape
-    columns = qkv_pieces[0].shape[1]
+    rows = pieces[0].shape[0]
     heads = columns // (3 * HEAD_DIM)
     inner = heads * HEAD_DIM
     return pl.pallas_call(
-        attend_backward,
+        functools.partial(attend_backward, columns),
         grid=(4,),
         in_specs=[
             SMEM,
@@ -482,38 +531,147 @@
             by_quarter((inner, seq)),
             by_quarter((heads, seq, seq)),
         ]
-        + [ANY] * (2 * N_PIECES),
+        + [ANY] * N_PIECES,
         out_specs=whole((seq, width)),
         out_shape=sds((seq, width), F32),
         scratch_shapes=[
-            pltpu.VMEM((4, width, columns), BF16),
-            pltpu.VMEM((4, inner, width), BF16),
+            pltpu.VMEM((4, rows, width), BF16),
             pltpu.VMEM((columns, seq), BF16),
-            pltpu.SemaphoreType.DMA((N_PIECES,)),
             pltpu.SemaphoreType.DMA((N_PIECES,)),
         ],
         compiler_params=params(),
+        cost_estimate=cost(16),
         name="attend_backward",
-    )(meta, grad_sum1, grad_low, flat, turned, att, prob, *qkv_pieces, *out_pieces)
+    )(meta, grad_sum1, grad_low, flat, turned, att, prob, *pieces)
+
+
+def prepare(meta, down, up, query, key, value, g1, s1, g2, s2, g3, s3, keep, send, lines, shard):
+    n_adapters, _, rank = down.shape
+    for i in range(n_adapters):
+        shard[0, :, i * rank : (i + 1) * rank] = down[i].astype(F32)
+        shard[1, :, i * rank : (i + 1) * rank] = up[i].astype(F32)
+    for i, ref in enumerate((query, key, value)):
+        shard[2 + i] = ref[...].astype(F32)
+    half = keep.shape[2]
+    mine = pl.multiple_of(meta[CORE] * half, LANES)
+    other = pl.multiple_of((1 - meta[CORE]) * half, LANES)
+    keep[...] = shard[:, :, pl.ds(mine, half)].astype(BF16)
+    send[...] = shard[:, :, pl.ds(other, half)].astype(BF16)
+    for i, ref in enumerate((g1, s1, g2, s2, g3, s3)):
+        lines[i : i + 1] = ref[...].reshape(1, -1)
+    lines[6:8] = jnp.zeros((2, lines.shape[1]), F32)
+
+
+def call_prepare(meta, down, up, query, key, value, *vectors):
+    rows, width = query.shape
+    half = sds((5, rows, width // 2), BF16)
+    return pl.pallas_call(
+        prepare,
+        in_specs=[SMEM] + [VMEM] * 11,
+        out_specs=[VMEM] * 3,
+        out_shape=[half, half, sds((8, width), F32)],
+        scratch_shapes=[pltpu.VMEM((5, rows, width), F32)],
+        compiler_params=params(),
+        cost_estimate=cost(1),
+        name="prepare",
+    )(meta, down, up, query, key, value, *vectors)
+
+
+def add_blocks(*blocks):
+    total = functools.reduce(jnp.add, (b.astype(F32) for b in blocks))
+    tail = total[-8:-4] + total[-4:]
+    return jnp.concatenate([total[:-8], split_lines(tail)], axis=0)
+
+
+def sum_cores(keep, got, p_keep, p_send, q_keep, q_send):
+    half = p_keep.shape[-1]
+    for x in range(2):
+        for y in range(2):
+
+            @pl.loop(0, 4)
+            def _(z, x=x, y=y):
+                total = add_blocks(keep[x, y, z], got[x, y, z]).astype(BF16)
+                (p_send if x else p_keep)[y, z] = total[:, :half]
+                (q_send if y else q_keep)[x, z] = total[:, half:]
+
+
+def sum_first(p_keep, p_got, q_keep, q_got, p2_keep, p2_send, q2_keep, q2_send):
+    @pl.loop(0, 4)
+    def _(z):
+        for out, index in ((p2_keep, 0), (p2_send, 1)):
+            out[z] = add_blocks(p_keep[index, z], p_got[index, z]).astype(BF16)
+        for out, index in ((q2_keep, 0), (q2_send, 1)):
+            out[z] = add_blocks(q_keep[index, z], q_got[index, z]).astype(BF16)
+
+
+def sum_second(p_keep, p_got, q_keep, q_got, *outs):
+    half = p_keep.shape[-1]
+    for z in range(4):
+        outs[z][:, :half] = add_blocks(p_keep[z], p_got[z]).astype(BF16)
+        outs[z][:, half:] = add_blocks(q_keep[z], q_got[z]).astype(BF16)
+
+
+def sum_last(n_adapters, keep, got1, got2, got3, query, key, value, gain, bias, mass):
+    total = add_blocks(keep[...], got1[...], got2[...], got3[...])
+    rows = query.shape[0]
+    for i, out in enumerate((query, key, value)):
+        out[...] = total[i * rows : (i + 1) * rows]
+    lines = total[-8:-4] + total[-4:]
+    gain[...] = lines[0]
+    bias[...] = lines[1]
+    mass[...] = lines[2, :n_adapters] / lines[2:3, n_adapters : n_adapters + 1].reshape(1)
+
+
+def small_call(body, name, out_shape, *operands):
+    return pl.pallas_call(
+        body,
+        in_specs=[VMEM] * len(operands),
+        out_specs=[VMEM] * len(out_shape),
+        out_shape=out_shape,
+        compiler_params=params(),
+        cost_estimate=cost(2),
+        name=name,
+    )(*operands)
+
+
+def sum_gradients(hops, keep, send, n_adapters):
+    block, width = keep.shape[3:]
+    half = width // 2
+    pair = [sds((2, 4, block, half), BF16)] * 4
+    single = [sds((4, block, half), BF16)] * 4
+    got = hops.flip(send, 1)
+    pk, ps, qk, qs = small_call(sum_cores, "sum_cores", pair, keep, got)
+    pg, qg = hops.flip(ps, ALONG_X), hops.flip(qs, ALONG_Y)
+    pk, ps, qk, qs = small_call(sum_first, "sum_first", single, pk, pg, qk, qg)
+    pg, qg = hops.flip(ps, ALONG_Y), hops.flip(qs, ALONG_X)
+    parts = small_call(sum_second, "sum_second", [sds((block, width), BF16)] * 4, pk, pg, qk, qg)
+    got = [hops.flip(part, z * ALONG_Z) for z, part in enumerate(parts) if z]
+    rows = (block - 8) // 3
+    outs = [sds((rows, width), F32)] * 3 + [sds((width,), F32)] * 2 + [sds((n_adapters,), F32)]
+    return small_call(
+        functools.partial(sum_last, n_adapters), "sum_last", outs, parts[0], *got
+    )
+
+
+ALONG_X, ALONG_Y, ALONG_Z = 2, 4, 8
 
 
 class Hops:
     def __init__(self, mesh):
         self.count = mesh.size
-        self.tensor = mesh.shape["tensor"]
-        self.dp = mesh.shape["dp"]
+        self.tiled = mesh.shape["dp"] == 8 and mesh.shape["tensor"] == 4
 
     def flip(self, array, bits):
         return lax.ppermute(array, AXES, [(i, i ^ bits) for i in range(self.count)])
 
 
-def frozen_pieces(hops, weight, parity):
-    half = weight.shape[0] // 2
-    mine = lax.dynamic_slice_in_dim(weight, parity * half, half, 0)
-    across = hops.flip(mine, 2)
-    around = hops.flip(across, hops.tensor)
-    other = hops.flip(weight, 1)
-    return (weight, other, across, around, hops.flip(across, 1), hops.flip(around, 1))
+def after(array, *others):
+    return lax.optimization_barrier((array, *others))[0]
+
+
+def half_of(block, parity):
+    half = block.shape[0] // 2
+    return lax.dynamic_slice_in_dim(block, parity * half, half, 0)
 
 
 def per_device(
@@ -538,60 +696,85 @@
     out_grad,
 ):
     n_adapters, rows, rank = adapter_down.shape
-    parity = lax.axis_index("dp") % 2
-    meta = jnp.stack([parity, lax.axis_index("tensor")]).astype(jnp.int32)
-    line = lambda v: v[None, :]
-
-    qkv_pieces = frozen_pieces(hops, qkv_weight, parity)
-    out_pieces = frozen_pieces(hops, attn_out_weight, parity)
-    in_pieces = frozen_pieces(hops, ffn_in_weight, parity)
-    up_pieces = frozen_pieces(hops, ffn_out_weight, parity)
-    shard = jnp.stack(
-        [
+    columns = qkv_weight.shape[1]
+    tensor, dp = lax.axis_index("tensor"), lax.axis_index("dp")
+    pair_y, pair_z = dp % 2, dp // 2 % 2
+    meta = jnp.stack([tensor % 2, tensor // 2, pair_y, pair_z, dp // 2, tensor]).astype(jnp.int32)
+    flip = hops.flip
+
+    attn = jnp.concatenate([qkv_weight.T, attn_out_weight], axis=0)
+    attn_x = flip(half_of(attn, pair_y), ALONG_X)
+    keep, send, lines = call_prepare(
+        meta,
+        adapter_down,
+        jnp.transpose(adapter_up, (0, 2, 1)),
+        merging_query,
+        merging_key,
+        merging_value,
+        norm1_gain,
+        norm1_bias,
+        norm2_gain,
+        norm2_bias,
+        merging_gain,
+        merging_bias,
+    )
+    if hops.tiled:
+        got = flip(send, 1)
+        tile = jnp.where(
+            tensor % 2 == 0,
+            jnp.concatenate([keep, got], axis=1),
+            jnp.concatenate([got, keep], axis=1),
+        )
+        tile_x = flip(tile, ALONG_X)
+        both = jnp.concatenate([tile, tile_x], axis=0)
+    attn_core = flip(attn, 1)
+    in_x = flip(half_of(after(ffn_in_weight, attn_core), pair_z), ALONG_X)
+    attn_y = flip(attn_x, ALONG_Y)
+    out_x = flip(half_of(after(ffn_out_weight, attn_x), pair_z), ALONG_X)
+    attn_pieces = (attn, attn_core, attn_x, attn_y, flip(attn_x, 1), flip(attn_y, 1))
+    in_z, out_z = flip(in_x, ALONG_Z), flip(out_x, ALONG_Z)
+    in_pieces = (ffn_in_weight, flip(ffn_in_weight, 1), in_x, in_z, flip(in_x, 1), flip(in_z, 1))
+    up_pieces = (
+        ffn_out_weight,
+        flip(ffn_out_weight, 1),
+        out_x,
+        out_z,
+        flip(out_x, 1),
+        flip(out_z, 1),
+    )
+    if hops.tiled:
+        by_z = [both] + [flip(both, z * ALONG_Z) for z in range(1, 4)]
+        mine = by_z + [flip(t, ALONG_Y) for t in by_z]
+        tiles = [t for own in mine for t in (own, flip(own, 1))]
+    else:
+        shard = [
             jnp.transpose(adapter_down, (1, 0, 2)).reshape(rows, n_adapters * rank),
             adapter_up.reshape(n_adapters * rank, rows).T,
             merging_query,
             merging_key,
             merging_value,
         ]
-    )
-    weights = lax.all_gather(shard, AXES, axis=1, tiled=True)
+        tiles = [lax.all_gather(jnp.stack(shard), AXES, axis=1, tiled=True)]
 
     flat, turned, att, prob, first, normed1, inv_std1 = call_attend_forward(
-        meta, doc_lengths, tokens, line(norm1_gain), line(norm1_bias), qkv_pieces, out_pieces
+        columns, meta, doc_lengths, tokens, lines, attn_pieces
     )
     slope, sums = call_ffn_forward(meta, first, in_pieces, up_pieces)
-    layer_out, grad_sum2, grad_sum2_low, grads, lines = call_merging(
-        n_adapters,
-        meta,
-        doc_lengths,
-        sums,
-        line(norm2_gain),
-        line(norm2_bias),
-        line(merging_gain),
-        line(merging_bias),
-        out_grad,
-        weights,
-        F32,
+    layer_out, grad_sum2, grad_sum2_low, *grads = call_merging(
+        n_adapters, hops.tiled, meta, doc_lengths, sums, lines, out_grad, tiles
     )
     grad_sum1, grad_sum1_low = call_ffn_backward(
-        meta, grad_sum2, grad_sum2_low, normed1, inv_std1, line(norm1_gain), slope, in_pieces, up_pieces
+        meta, grad_sum2, grad_sum2_low, normed1, inv_std1, lines, slope, in_pieces, up_pieces
     )
     input_grad = call_attend_backward(
-        meta, grad_sum1, grad_sum1_low, flat, turned, att, prob, qkv_pieces, out_pieces
-    )
-    grads = lax.psum_scatter(grads, AXES, scatter_dimension=1, tiled=True)
-    lines = lax.psum(lines, AXES)
-    return (
-        layer_out,
-        input_grad,
-        grads[0],
-        grads[1],
-        grads[2],
-        lines[0],
-        lines[1],
-        lines[2, :n_adapters] / lines[2, n_adapters],
-    )
+        columns, meta, grad_sum1, grad_sum1_low, flat, turned, att, prob, attn_pieces
+    )
+    if hops.tiled:
+        return (layer_out, input_grad, *sum_gradients(hops, *grads, n_adapters))
+    squares = lax.psum_scatter(grads[0], AXES, scatter_dimension=1, tiled=True)
+    sums = lax.psum(grads[1], AXES)
+    mass = sums[2, :n_adapters] / sums[2, n_adapters]
+    return (layer_out, input_grad, squares[0], squares[1], squares[2], sums[0], sums[1], mass)
 
 
 def solution(mesh):

time: 288 us -> 253 us (0.88)
  blocking collectives: 40 us -> 0 us
  Pallas kernels: 80 us -> 95.6 us
  starting transfers between devices: 13.1 us -> 27.6 us
  between operations: 14.3 us -> 1.04 us
  local copies, waits for them, and re-layouts: 20.7 us -> 9.32 us
    reduce_scatter x1 -> x0, waiting for transfers between devices: 45.3 us -> none  [per_device(): grads = lax.psum_scatter(grads, AXES, scatter_dimension=1, tiled=True)]
    ppermute x20 -> x40, waiting for transfers between devices: 72.4 us -> 116 us  [flip(): return lax.ppermute(array, AXES, [(i, i ^ bits) for i in range(self.count)])]
    psum x1 -> x0, blocking collectives: 40 us -> none  [per_device(): lines = lax.psum(lines, AXES)]
    pallas_call x3 -> x8, Pallas kernels: 55.4 us -> 71.1 us  [the longest x1 22.3 us: call_merging(): pl.pallas_call(functools.partial(merging, n_adapters, tiled), in_specs=[S...]
    ppermute x20 -> x40, starting transfers between devices: 13 us -> 27.6 us  [flip(): return lax.ppermute(array, AXES, [(i, i ^ bits) for i in range(self.count)])]
    broadcast_in_dim x6 -> x0, local copies, waits for them, and re-layouts: 3.5 us -> none  [per_device(): line = lambda v: v[None, :]]
    unnamed x44 -> x60, local copies, waits for them, and re-layouts: 7.53 us -> 7.5 us
  transfers between devices with their start and end apart: 22 -> 40, of which waited for: 7 -> 13; matrix products, arithmetic and copies ran while one was open for 4% -> 1% of each run, Pallas kernels for 21% -> 25%
where the time goes in v2:
time: 253 us; the launch traced here: 252 us
  waiting for transfers between devices  116 us (46%)
  Pallas kernels  95.6 us (38%)
  starting transfers between devices  27.6 us (11%)
  local copies, waits for them, and re-layouts  9.32 us (4%)
  other arithmetic  3.01 us (1%)
    ppermute x40, waiting for transfers between devices, flip(): return lax.ppermute(array, AXES, [(i, i ^ bits) for i in range(self.count)])  116 us
    ppermute x40, starting transfers between devices, flip(): return lax.ppermute(array, AXES, [(i, i ^ bits) for i in range(self.count)])  27.6 us
    pallas_call x1, Pallas kernels, call_merging(): pl.pallas_call(functools.partial(merging, n_adapters, tiled), in_specs=[S...  22.3 us
    pallas_call x1, Pallas kernels, call_attend_forward(): pl.pallas_call(functools.partial(attend_forward, columns), grid=(4,), in_...  18.3 us
    pallas_call x1, Pallas kernels, call_attend_backward(): pl.pallas_call(functools.partial(attend_backward, columns), grid=(4,), in...  17.9 us
    pallas_call x1, Pallas kernels, call_ffn_backward(): pl.pallas_call(ffn_backward, grid=(4,), in_specs=[SMEM, whole((seq, width...  12.8 us
    pallas_call x1, Pallas kernels, call_ffn_forward(): pl.pallas_call(ffn_forward, grid=(4,), in_specs=[SMEM, whole((seq, width)...  11.6 us
    pallas_call x4, Pallas kernels, small_call(): pl.pallas_call(body, in_specs=[VMEM] * len(operands), out_specs=[VMEM] *...  10.8 us
  transfers between devices with their start and end apart: 40, of which 13 were waited for; matrix products, arithmetic and copies ran while one was open for 1% of the time, Pallas kernels for 25%

profile of v2, /device:TPU:0, one launch (start us, length us, event | category | flops | bytes accessed | tf_op | source)
XLA Modules:
  0.0 252.1 jit_solution(15672265745860995075)
XLA Ops:
  3.1 2.6 %collective-permute-start.1 = (bf16[384,768]{1,0:T(8,128)(2,1)S(1)}, bf16[384,768]{1,0:T(8,128)(2,1)}, u32[]{:S(2)}, u32[]{:S(2)}) collective-permute-start(bf16[384,768]{1,0:T(8,128)(2,1)S(1)} %fusion), channel_id=1, source_target_pairs={{0,2},{1,3},{2,0},{3,1},{4,6},{5,7},{6,4},{7,5},{8,10},{9,11},{10,... | collective-permute-start | bytes 1769480 | tf_op jit(solution)/shard_map/ppermute | solution.py:665
  11.0 12.6 %collective-permute-done.16 = bf16[5,48,384]{2,1,0:T(8,128)(2,1)S(1)} collective-permute-done((bf16[5,48,384]{2,1,0:T(8,128)(2,1)S(1)}, bf16[5,48,384]{2,1,0:T(8,128)(2,1)S(1)}, u32[]{:S(2)}, u32[]{:S(2)}) %collective-permute-start.16) | collective-permute-done | bytes 184352 | tf_op jit(solution)/shard_map/ppermute | solution.py:665
  23.7 1.8 collective-permute-start.24
  25.6 3.6 %collective-permute-start.22 = (bf16[10,48,384]{2,1,0:T(8,128)(2,1)S(1)}, bf16[10,48,384]{2,1,0:T(8,128)(2,1)}, u32[]{:S(2)}, u32[]{:S(2)}) collective-permute-start(bf16[10,48,384]{2,1,0:T(8,128)(2,1)S(1)} %pad_maximum_fusion.1.refs_0_), channel_id=1, source_target_pairs={{0,24},{1,25},{2,26},{3,27},{4,28},{5,29},{6,30},{7,31},{8,16},{9,... | collective-permute-start | bytes 1105928 | tf_op jit(solution)/shard_map/ppermute | solution.py:665
  29.9 4.3 %collective-permute-done.24.refs_8_ = bf16[10,48,384]{2,1,0:T(8,128)(2,1)} collective-permute-done((bf16[10,48,384]{2,1,0:T(8,128)(2,1)S(1)}, bf16[10,48,384]{2,1,0:T(8,128)(2,1)}, u32[]{:S(2)}, u32[]{:S(2)}) %collective-permute-start.24) | collective-permute-done | bytes 368672 | tf_op jit(solution)/shard_map/ppermute | solution.py:665
  34.2 4.9 %collective-permute-done.22.refs_6_ = bf16[10,48,384]{2,1,0:T(8,128)(2,1)} collective-permute-done((bf16[10,48,384]{2,1,0:T(8,128)(2,1)S(1)}, bf16[10,48,384]{2,1,0:T(8,128)(2,1)}, u32[]{:S(2)}, u32[]{:S(2)}) %collective-permute-start.22) | collective-permute-done | bytes 368672 | tf_op jit(solution)/shard_map/ppermute | solution.py:665
  39.1 21.0 %collective-permute-done.20.refs_4_ = bf16[10,48,384]{2,1,0:T(8,128)(2,1)S(1)} collective-permute-done((bf16[10,48,384]{2,1,0:T(8,128)(2,1)S(1)}, bf16[10,48,384]{2,1,0:T(8,128)(2,1)S(1)}, u32[]{:S(2)}, u32[]{:S(2)}) %collective-permute-start.20) | collective-permute-done | bytes 368672 | tf_op jit(solution)/shard_map/ppermute | solution.py:665
  65.8 6.2 %collective-permute-done.30.refs_14_ = bf16[10,48,384]{2,1,0:T(8,128)(2,1)} collective-permute-done((bf16[10,48,384]{2,1,0:T(8,128)(2,1)}, bf16[10,48,384]{2,1,0:T(8,128)(2,1)}, u32[]{:S(2)}, u32[]{:S(2)}) %collective-permute-start.30) | collective-permute-done | bytes 368672 | tf_op jit(solution)/shard_map/ppermute | solution.py:665
  74.0 5.8 %collective-permute-done.28.refs_12_ = bf16[10,48,384]{2,1,0:T(8,128)(2,1)S(1)} collective-permute-done((bf16[10,48,384]{2,1,0:T(8,128)(2,1)}, bf16[10,48,384]{2,1,0:T(8,128)(2,1)S(1)}, u32[]{:S(2)}, u32[]{:S(2)}) %collective-permute-start.28) | collective-permute-done | bytes 368672 | tf_op jit(solution)/shard_map/ppermute | solution.py:665
  80.3 18.1 %collective-permute-done.26.refs_10_ = bf16[10,48,384]{2,1,0:T(8,128)(2,1)S(1)} collective-permute-done((bf16[10,48,384]{2,1,0:T(8,128)(2,1)S(1)}, bf16[10,48,384]{2,1,0:T(8,128)(2,1)S(1)}, u32[]{:S(2)}, u32[]{:S(2)}) %collective-permute-start.26) | collective-permute-done | bytes 368672 | tf_op jit(solution)/shard_map/ppermute | solution.py:665
  101.2 13.7 %collective-permute-done.12.refs_11_.refs_16_ = bf16[384,768]{1,0:T(8,128)(2,1)} collective-permute-done((bf16[384,768]{1,0:T(8,128)(2,1)}, bf16[384,768]{1,0:T(8,128)(2,1)}, u32[]{:S(2)}, u32[]{:S(2)}) %collective-permute-start.12) | collective-permute-done | bytes 589856 | tf_op jit(solution)/shard_map/ppermute | solution.py:665
  116.2 10.8 %collective-permute-done.7.refs_5_.refs_10_ = bf16[384,768]{1,0:T(8,128)(2,1)} collective-permute-done((bf16[384,768]{1,0:T(8,128)(2,1)}, bf16[384,768]{1,0:T(8,128)(2,1)}, u32[]{:S(2)}, u32[]{:S(2)}) %collective-permute-start.7) | collective-permute-done | bytes 589856 | tf_op jit(solution)/shard_map/ppermute | solution.py:665
  127.1 18.3 %attend_forward.1 = (bf16[4,512,576]{2,1,0:T(8,128)(2,1)}, bf16[4,576,512]{2,1,0:T(8,128)(2,1)}, bf16[4,192,512]{2,1,0:T(8,128)(2,1)}, bf16[4,3,512,512]{3,2,1,0...) custom-call(s32[6]{0:T(128)} %stack.27.meta.refs_0_, s32[4,8]{1,0:T(4,128)} %lengths.1, ...), custom_call_target="tpu_custom_call" | custom-call | flops 17600000000 | bytes 1048576 | tf_op jit(solution)/shard_map/attend_forward/pallas_call | solution.py:175
  147.4 11.6 %ffn_forward.1 = (bf16[4,512,768]{2,1,0:T(8,128)(2,1)}, f32[512,768]{1,0:T(8,128)}) custom-call(s32[6]{0:T(128)} %stack.27.meta.refs_0_, f32[512,768]{1,0:T(8,128)} %get-tuple-element.48.refs_1_, bf16[768,768]{1,0:T(8,128)(2,1)} %refs_7_.1, bf16[768,768]{1,0:T(8,128)(2,1)} %copy-done.7, bf16[384,768]{1,0:T(8,128)(2,1)} %collective-permute-done.6.refs_4_.refs_9_, ...), custom_call_target="tpu_custom_call" | custom-call | flops 12099999744 | bytes 1048576 | tf_op jit(solution)/shard_map/ffn_forward/pallas_call | solution.py:235
  160.3 22.3 %merging.1 = (f32[512,768]{1,0:T(8,128)}, f32[512,768]{1,0:T(8,128)}, bf16[512,768]{1,0:T(8,128)(2,1)}, bf16[2,2,4,80,768]{4,3,2,1,0:T(8,128)(2,1)}, bf16[2,2,4,80,768]{4,3,2,1,0:T(8,128)(2,1)}) custom-call(s32[6]{0:T(128)} %stack.27.meta.refs_0_, s32[4,8]{1,0:T(4,128)} %lengths.1, f32[512,768]{1,0:T(8,128)} %get-tuple-element.51.sums, ...), custom_call_target="tpu_custom_call" | custom-call | flops 19800000512 | bytes 1048576 | tf_op jit(solution)/shard_map/merging/pallas_call | solution.py:412
  182.7 4.1 %collective-permute-done.32.got = bf16[2,2,4,80,768]{4,3,2,1,0:T(8,128)(2,1)S(1)} collective-permute-done((bf16[2,2,4,80,768]{4,3,2,1,0:T(8,128)(2,1)}, bf16[2,2,4,80,768]{4,3,2,1,0:T(8,128)(2,1)S(1)}, u32[]{:S(2)}, u32[]{:S(2)}) %collective-permute-start.32) | collective-permute-done | bytes 1966112 | tf_op jit(solution)/shard_map/ppermute | solution.py:665
  188.1 4.1 %sum_cores.1 = (bf16[2,4,80,384]{3,2,1,0:T(8,128)(2,1)}, bf16[2,4,80,384]{3,2,1,0:T(8,128)(2,1)}, bf16[2,4,80,384]{3,2,1,0:T(8,128)(2,1)}, bf16[2,4,80,384]{3,2,1,0:T(8,128)(2,1)}) custom-call(bf16[2,2,4,80,768]{4,3,2,1,0:T(8,128)(2,1)} %get-tuple-element.66.keep, bf16[2,2,4,80,768]{4,3,2,1,0:T(8,128)(2,1)} %copy-done.6), custom_call_target="tpu_custom_call" | custom-call | flops 2200000000 | bytes 1048576 | tf_op jit(solution)/shard_map/sum_cores/pallas_call | solution.py:626
  194.2 11.5 %collective-permute-done.33.p_got = bf16[2,4,80,384]{3,2,1,0:T(8,128)(2,1)S(1)} collective-permute-done((bf16[2,4,80,384]{3,2,1,0:T(8,128)(2,1)}, bf16[2,4,80,384]{3,2,1,0:T(8,128)(2,1)S(1)}, u32[]{:S(2)}, u32[]{:S(2)}) %collective-permute-start.33) | collective-permute-done | bytes 491552 | tf_op jit(solution)/shard_map/ppermute | solution.py:665
  207.7 2.7 %sum_first.1 = (bf16[4,80,384]{2,1,0:T(8,128)(2,1)}, bf16[4,80,384]{2,1,0:T(8,128)(2,1)}, bf16[4,80,384]{2,1,0:T(8,128)(2,1)}, bf16[4,80,384]{2,1,0:T(8,128)(2,1)}) custom-call(bf16[2,4,80,384]{3,2,1,0:T(8,128)(2,1)} %get-tuple-element.68.p_keep, bf16[2,4,80,384]{3,2,1,0:T(8,128)(2,1)} %copy-done.13, bf16[2,4,80,384]{3,2,1,0:T(8,128)(2,1)} %get-tuple-element.70.q_keep, ...), custom_call_target="tpu_custom_call" | custom-call | flops 2200000000 | bytes 1048576 | tf_op jit(solution)/shard_map/sum_first/pallas_call | solution.py:626
  211.5 12.8 %ffn_backward.1 = (f32[512,768]{1,0:T(8,128)}, bf16[512,768]{1,0:T(8,128)(2,1)}) custom-call(s32[6]{0:T(128)} %stack.27.meta.refs_0_, f32[512,768]{1,0:T(8,128)} %get-tuple-element.55.refs_1_, bf16[512,768]{1,0:T(8,128)(2,1)} %get-tuple-element.56.refs_2_, f32[512,768]{1,0:T(8,128)} %get-tuple-element.57.refs_3_, f32[512,1]{1,0:T(8,128)} %get-tuple-element.58.refs_4_, ...), custom_call_target="tpu_custom_call" | custom-call | flops 13200000000 | bytes 1048576 | tf_op jit(solution)/shard_map/ffn_backward/pallas_call | solution.py:457
  225.1 2.2 sum_second.1
  227.6 2.1 collective-permute-start.38
  229.7 2.0 collective-permute-start.39
  231.7 17.9 %attend_backward.1 = f32[512,768]{1,0:T(8,128)} custom-call(s32[6]{0:T(128)} %stack.27.meta.refs_0_, f32[512,768]{1,0:T(8,128)} %get-tuple-element.60.refs_1_, bf16[512,768]{1,0:T(8,128)(2,1)} %get-tuple-element.61.refs_2_, bf16[4,512,576]{2,1,0:T(8,128)(2,1)} %get-tuple-element.62.refs_3_, bf16[4,576,512]{2,1,0:T(8,128)(2,1)} %get-tuple-element.63.refs_4_, ...), custom_call_target="tpu_custom_call" | custom-call | flops 17600000000 | bytes 1048576 | tf_op jit(solution)/shard_map/attend_backward/pallas_call | solution.py:522
  (133 shorter events, 34.0 us)
Async XLA Ops:
  2.1 58.8 %collective-permute-start = (bf16[768,768]{1,0:T(8,128)(2,1)S(1)}, bf16[768,768]{1,0:T(8,128)(2,1)}, u32[]{:S(2)}, u32[]{:S(2)}) collective-permute-start(bf16[768,768]{1,0:T(8,128)(2,1)S(1)} %pad_maximum_fusion.refs_4_.refs_7_), channel_id=1, source_target_pairs={{0,1},{1,0},{2,3},{3,2},{4,5},{5,4},{6,7},{7,6},{8,9},{9,8},{10,11... | collective-permute-start | bytes 3538952 | tf_op jit(solution)/shard_map/ppermute | solution.py:665
  3.1 26.0 %collective-permute-start.1 = (bf16[384,768]{1,0:T(8,128)(2,1)S(1)}, bf16[384,768]{1,0:T(8,128)(2,1)}, u32[]{:S(2)}, u32[]{:S(2)}) collective-permute-start(bf16[384,768]{1,0:T(8,128)(2,1)S(1)} %fusion), channel_id=1, source_target_pairs={{0,2},{1,3},{2,0},{3,1},{4,6},{5,7},{6,4},{7,5},{8,10},{9,11},{10,... | collective-permute-start | bytes 1769480 | tf_op jit(solution)/shard_map/ppermute | solution.py:665
  29.2 31.0 %collective-permute-start.20 = (bf16[10,48,384]{2,1,0:T(8,128)(2,1)S(1)}, bf16[10,48,384]{2,1,0:T(8,128)(2,1)S(1)}, u32[]{:S(2)}, u32[]{:S(2)}) collective-permute-start(bf16[10,48,384]{2,1,0:T(8,128)(2,1)S(1)} %pad_maximum_fusion.1.refs_0_), channel_id=1, source_target_pairs={{0,16},{1,17},{2,18},{3,19},{4,20},{5,21},{6,22},{7,23},{8,24},{9,... | collective-permute-start | bytes 1105928 | tf_op jit(solution)/shard_map/ppermute | solution.py:665
  29.2 31.5 %collective-permute-start.18 = (bf16[10,48,384]{2,1,0:T(8,128)(2,1)S(1)}, bf16[10,48,384]{2,1,0:T(8,128)(2,1)S(1)}, u32[]{:S(2)}, u32[]{:S(2)}) collective-permute-start(bf16[10,48,384]{2,1,0:T(8,128)(2,1)S(1)} %pad_maximum_fusion.1.refs_0_), channel_id=1, source_target_pairs={{0,8},{1,9},{2,10},{3,11},{4,12},{5,13},{6,14},{7,15},{8,0},{9,1},... | collective-permute-start | bytes 1105928 | tf_op jit(solution)/shard_map/ppermute | solution.py:665
  34.2 29.9 %collective-permute-start.17 = (bf16[10,48,384]{2,1,0:T(8,128)(2,1)S(1)}, bf16[10,48,384]{2,1,0:T(8,128)(2,1)}, u32[]{:S(2)}, u32[]{:S(2)}) collective-permute-start(bf16[10,48,384]{2,1,0:T(8,128)(2,1)S(1)} %pad_maximum_fusion.1.refs_0_), channel_id=1, source_target_pairs={{0,1},{1,0},{2,3},{3,2},{4,5},{5,4},{6,7},{7,6},{8,9},{9,8},{10,11... | collective-permute-start | bytes 1105928 | tf_op jit(solution)/shard_map/ppermute | solution.py:665
  39.1 25.1 %collective-permute-start.25 = (bf16[10,48,384]{2,1,0:T(8,128)(2,1)}, bf16[10,48,384]{2,1,0:T(8,128)(2,1)}, u32[]{:S(2)}, u32[]{:S(2)}) collective-permute-start(bf16[10,48,384]{2,1,0:T(8,128)(2,1)} %collective-permute-done.24.refs_8_), channel_id=1, source_target_pairs={{0,1},{1,0},{2,3},{3,2},{4,5},{5,4},{6,7},{7,6},{8,9},{9,8},{10,11... | collective-permute-start | bytes 1105928 | tf_op jit(solution)/shard_map/ppermute | solution.py:665
  61.6 18.2 %collective-permute-start.28 = (bf16[10,48,384]{2,1,0:T(8,128)(2,1)}, bf16[10,48,384]{2,1,0:T(8,128)(2,1)S(1)}, u32[]{:S(2)}, u32[]{:S(2)}) collective-permute-start(bf16[10,48,384]{2,1,0:T(8,128)(2,1)} %copy-done.15), channel_id=1, source_target_pairs={{0,4},{1,5},{2,6},{3,7},{4,0},{5,1},{6,2},{7,3},{8,12},{9,13},{10,... | collective-permute-start | bytes 1105928 | tf_op jit(solution)/shard_map/ppermute | solution.py:665
  64.1 36.7 %collective-permute-start.5 = (bf16[768,768]{1,0:T(8,128)(2,1)S(1)}, bf16[768,768]{1,0:T(8,128)(2,1)S(1)}, u32[]{:S(2)}, u32[]{:S(2)}) collective-permute-start(bf16[768,768]{1,0:T(8,128)(2,1)S(1)} %copy-done.4), channel_id=1, source_target_pairs={{0,1},{1,0},{2,3},{3,2},{4,5},{5,4},{6,7},{7,6},{8,9},{9,8},{10,11... | collective-permute-start | bytes 3538952 | tf_op jit(solution)/shard_map/ppermute | solution.py:665
  64.2 34.2 %collective-permute-start.11 = (bf16[384,768]{1,0:T(8,128)(2,1)S(1)}, bf16[384,768]{1,0:T(8,128)(2,1)}, u32[]{:S(2)}, u32[]{:S(2)}) collective-permute-start(bf16[384,768]{1,0:T(8,128)(2,1)S(1)} %constant_dynamic-slice_fusion), channel_id=1, source_target_pairs={{0,2},{1,3},{2,0},{3,1},{4,6},{5,7},{6,4},{7,5},{8,10},{9,11},{10,... | collective-permute-start | bytes 1769480 | tf_op jit(solution)/shard_map/ppermute | solution.py:665
  72.0 27.1 %collective-permute-start.2 = (bf16[384,768]{1,0:T(8,128)(2,1)}, bf16[384,768]{1,0:T(8,128)(2,1)S(1)}, u32[]{:S(2)}, u32[]{:S(2)}) collective-permute-start(bf16[384,768]{1,0:T(8,128)(2,1)} %collective-permute-done.1.refs_6_.refs_9_), channel_id=1, source_target_pairs={{0,4},{1,5},{2,6},{3,7},{4,0},{5,1},{6,2},{7,3},{8,12},{9,13},{10,... | collective-permute-start | bytes 1769480 | tf_op jit(solution)/shard_map/ppermute | solution.py:665
  72.5 26.6 %collective-permute-start.6 = (bf16[384,768]{1,0:T(8,128)(2,1)S(1)}, bf16[384,768]{1,0:T(8,128)(2,1)}, u32[]{:S(2)}, u32[]{:S(2)}) collective-permute-start(bf16[384,768]{1,0:T(8,128)(2,1)S(1)} %constant_dynamic-slice_fusion.1), channel_id=1, source_target_pairs={{0,2},{1,3},{2,0},{3,1},{4,6},{5,7},{6,4},{7,5},{8,10},{9,11},{10,... | collective-permute-start | bytes 1769480 | tf_op jit(solution)/shard_map/ppermute | solution.py:665
  79.8 18.6 %collective-permute-start.26 = (bf16[10,48,384]{2,1,0:T(8,128)(2,1)S(1)}, bf16[10,48,384]{2,1,0:T(8,128)(2,1)S(1)}, u32[]{:S(2)}, u32[]{:S(2)}) collective-permute-start(bf16[10,48,384]{2,1,0:T(8,128)(2,1)S(1)} %copy-done.17), channel_id=1, source_target_pairs={{0,4},{1,5},{2,6},{3,7},{4,0},{5,1},{6,2},{7,3},{8,12},{9,13},{10,... | collective-permute-start | bytes 1105928 | tf_op jit(solution)/shard_map/ppermute | solution.py:665
  98.4 16.5 %collective-permute-start.12 = (bf16[384,768]{1,0:T(8,128)(2,1)}, bf16[384,768]{1,0:T(8,128)(2,1)}, u32[]{:S(2)}, u32[]{:S(2)}) collective-permute-start(bf16[384,768]{1,0:T(8,128)(2,1)} %collective-permute-done.11.refs_10_.refs_15_), channel_id=1, source_target_pairs={{0,8},{1,9},{2,10},{3,11},{4,12},{5,13},{6,14},{7,15},{8,0},{9,1},... | collective-permute-start | bytes 1769480 | tf_op jit(solution)/shard_map/ppermute | solution.py:665
  99.1 15.8 %collective-permute-start.4 = (bf16[384,768]{1,0:T(8,128)(2,1)S(1)}, bf16[384,768]{1,0:T(8,128)(2,1)S(1)}, u32[]{:S(2)}, u32[]{:S(2)}) collective-permute-start(bf16[384,768]{1,0:T(8,128)(2,1)S(1)} %collective-permute-done.2.refs_7_.refs_10_), channel_id=1, source_target_pairs={{0,1},{1,0},{2,3},{3,2},{4,5},{5,4},{6,7},{7,6},{8,9},{9,8},{10,11... | collective-permute-start | bytes 1769480 | tf_op jit(solution)/shard_map/ppermute | solution.py:665
  99.1 28.0 %collective-permute-start.7 = (bf16[384,768]{1,0:T(8,128)(2,1)}, bf16[384,768]{1,0:T(8,128)(2,1)}, u32[]{:S(2)}, u32[]{:S(2)}) collective-permute-start(bf16[384,768]{1,0:T(8,128)(2,1)} %collective-permute-done.6.refs_4_.refs_9_), channel_id=1, source_target_pairs={{0,8},{1,9},{2,10},{3,11},{4,12},{5,13},{6,14},{7,15},{8,0},{9,1},... | collective-permute-start | bytes 1769480 | tf_op jit(solution)/shard_map/ppermute | solution.py:665
  100.7 44.7 %collective-permute-start.10 = (bf16[768,768]{1,0:T(8,128)(2,1)S(1)}, bf16[768,768]{1,0:T(8,128)(2,1)S(1)}, u32[]{:S(2)}, u32[]{:S(2)}) collective-permute-start(bf16[768,768]{1,0:T(8,128)(2,1)S(1)} %copy-done.5), channel_id=1, source_target_pairs={{0,1},{1,0},{2,3},{3,2},{4,5},{5,4},{6,7},{7,6},{8,9},{9,8},{10,11... | collective-permute-start | bytes 3538952 | tf_op jit(solution)/shard_map/ppermute | solution.py:665
  100.9 45.2 %collective-permute-start.13 = (bf16[384,768]{1,0:T(8,128)(2,1)}, bf16[384,768]{1,0:T(8,128)(2,1)S(1)}, u32[]{:S(2)}, u32[]{:S(2)}) collective-permute-start(bf16[384,768]{1,0:T(8,128)(2,1)} %collective-permute-done.11.refs_10_.refs_15_), channel_id=1, source_target_pairs={{0,1},{1,0},{2,3},{3,2},{4,5},{5,4},{6,7},{7,6},{8,9},{9,8},{10,11... | collective-permute-start | bytes 1769480 | tf_op jit(solution)/shard_map/ppermute | solution.py:665
  114.9 31.7 %collective-permute-start.8 = (bf16[384,768]{1,0:T(8,128)(2,1)}, bf16[384,768]{1,0:T(8,128)(2,1)S(1)}, u32[]{:S(2)}, u32[]{:S(2)}) collective-permute-start(bf16[384,768]{1,0:T(8,128)(2,1)} %collective-permute-done.6.refs_4_.refs_9_), channel_id=1, source_target_pairs={{0,1},{1,0},{2,3},{3,2},{4,5},{5,4},{6,7},{7,6},{8,9},{9,8},{10,11... | collective-permute-start | bytes 1769480 | tf_op jit(solution)/shard_map/ppermute | solution.py:665
  115.7 30.4 %collective-permute-start.14 = (bf16[384,768]{1,0:T(8,128)(2,1)}, bf16[384,768]{1,0:T(8,128)(2,1)}, u32[]{:S(2)}, u32[]{:S(2)}) collective-permute-start(bf16[384,768]{1,0:T(8,128)(2,1)} %collective-permute-done.12.refs_11_.refs_16_), channel_id=1, source_target_pairs={{0,1},{1,0},{2,3},{3,2},{4,5},{5,4},{6,7},{7,6},{8,9},{9,8},{10,11... | collective-permute-start | bytes 1769480 | tf_op jit(solution)/shard_map/ppermute | solution.py:665
  127.1 19.6 %collective-permute-start.9 = (bf16[384,768]{1,0:T(8,128)(2,1)}, bf16[384,768]{1,0:T(8,128)(2,1)}, u32[]{:S(2)}, u32[]{:S(2)}) collective-permute-start(bf16[384,768]{1,0:T(8,128)(2,1)} %collective-permute-done.7.refs_5_.refs_10_), channel_id=1, source_target_pairs={{0,1},{1,0},{2,3},{3,2},{4,5},{5,4},{6,7},{7,6},{8,9},{9,8},{10,11... | collective-permute-start | bytes 1769480 | tf_op jit(solution)/shard_map/ppermute | solution.py:665
  210.4 13.9 %collective-permute-start.35 = (bf16[4,80,384]{2,1,0:T(8,128)(2,1)}, bf16[4,80,384]{2,1,0:T(8,128)(2,1)S(1)}, u32[]{:S(2)}, u32[]{:S(2)}) collective-permute-start(bf16[4,80,384]{2,1,0:T(8,128)(2,1)} %get-tuple-element.73), channel_id=1, source_target_pairs={{0,4},{1,5},{2,6},{3,7},{4,0},{5,1},{6,2},{7,3},{8,12},{9,13},{10,... | collective-permute-start | bytes 737288 | tf_op jit(solution)/shard_map/ppermute | solution.py:665
  227.3 22.3 %collective-permute-start.37 = (bf16[80,768]{1,0:T(8,128)(2,1)}, bf16[80,768]{1,0:T(8,128)(2,1)S(1)}, u32[]{:S(2)}, u32[]{:S(2)}) collective-permute-start(bf16[80,768]{1,0:T(8,128)(2,1)} %get-tuple-element.77), channel_id=1, source_target_pairs={{0,8},{1,9},{2,10},{3,11},{4,12},{5,13},{6,14},{7,15},{8,0},{9,1},... | collective-permute-start | bytes 368648 | tf_op jit(solution)/shard_map/ppermute | solution.py:665
  227.6 22.0 %collective-permute-start.38 = (bf16[80,768]{1,0:T(8,128)(2,1)}, bf16[80,768]{1,0:T(8,128)(2,1)S(1)}, u32[]{:S(2)}, u32[]{:S(2)}) collective-permute-start(bf16[80,768]{1,0:T(8,128)(2,1)} %get-tuple-element.78), channel_id=1, source_target_pairs={{0,16},{1,17},{2,18},{3,19},{4,20},{5,21},{6,22},{7,23},{8,24},{9,... | collective-permute-start | bytes 368648 | tf_op jit(solution)/shard_map/ppermute | solution.py:665
  229.7 20.0 %collective-permute-start.39 = (bf16[80,768]{1,0:T(8,128)(2,1)}, bf16[80,768]{1,0:T(8,128)(2,1)S(1)}, u32[]{:S(2)}, u32[]{:S(2)}) collective-permute-start(bf16[80,768]{1,0:T(8,128)(2,1)} %get-tuple-element.79), channel_id=1, source_target_pairs={{0,24},{1,25},{2,26},{3,27},{4,28},{5,29},{6,30},{7,31},{8,16},{9,... | collective-permute-start | bytes 368648 | tf_op jit(solution)/shard_map/ppermute | solution.py:665
  (46 other events, 544.5 us)
